TPU v7x, 256 devices: a whole 4x4x8 slice. The times are simulated.
256 devices in a mesh: wide: 64 (over x, y_hi, z), narrow: 4 (over y_lo, core).
Axes of the slice: x: 4, y: 4 (y_hi: 2, y_lo: 2; y = y_hi * 2 + y_lo), z: 8, core: 2. Of those that a mesh axis runs over, the one named last changes fastest.
Arguments:
- image_features: bfloat16 [49152, 1152], P(('wide', 'narrow')), may hold values from -6 to 6
- text_features: bfloat16 [49152, 1152], P(('wide', 'narrow')), may hold values from -6 to 6
- image_weight: bfloat16 [1152, 1152], replicated, may hold values from -0.1875 to 0.1875
- text_weight: bfloat16 [1152, 1152], replicated, may hold values from -0.1875 to 0.1875
- partner: int32 [64, 768], P('wide', 'narrow'), may hold values from 0 to 767, each once within a row
Outputs:
- image_feature_grad: bfloat16 [49152, 1152], P(('wide', 'narrow'))
- text_feature_grad: bfloat16 [49152, 1152], P(('wide', 'narrow'))
- image_weight_grad: float32 [1152, 1152], P('wide', 'narrow')
- text_weight_grad: float32 [1152, 1152], P('wide', 'narrow')
Inputs may be any that keep to these rules, and one draw needn't show every extreme that they name: `partner`: each row is a permutation: every caption of a group belongs to exactly one image of that group.
All inputs are finite; a program needn't handle non-finite values.
Results may differ from a plain program's by a relative error of at most 0.007.
Values may be sent and summed in bfloat16 or wider, within the bound.
A program may use at most 128 MiB of HBM per device.

v0:
```python
import jax
import jax.numpy as jnp
from jax import lax
from jax.sharding import PartitionSpec as P

logit_scale = 10.0
logit_bias = -2.0
norm_eps = 1e-06


def embed(features, weight):
    proj = jnp.dot(features, weight, preferred_element_type=jnp.float32)
    inverse = lax.rsqrt(jnp.sum(proj * proj, axis=1, keepdims=True) + norm_eps)
    return (proj, inverse, (proj * inverse).astype(jnp.bfloat16))


def pair_terms(left, right, match):
    logits = (
        logit_scale
        * lax.dot_general(left, right, (((1,), (1,)), ((), ())), preferred_element_type=jnp.float32)
        + logit_bias
    )
    signs = jnp.where(match, 1.0, -1.0).astype(jnp.float32)
    return (-logit_scale * signs * jax.nn.sigmoid(-signs * logits)).astype(jnp.bfloat16)


def proj_backward(proj, inverse, grad):
    along = jnp.sum(proj * grad, axis=1, keepdims=True)
    return (inverse * grad - proj * (inverse * inverse * inverse) * along).astype(jnp.bfloat16)


def local(image_features, text_features, image_weight, text_weight, partner):
    rows = image_features.shape[0]
    partner_row = partner[0]
    my_columns = lax.axis_index("narrow") * rows + jnp.arange(rows, dtype=jnp.int32)
    image_proj, image_inv, image_emb = embed(image_features, image_weight)
    text_proj, text_inv, text_emb = embed(text_features, text_weight)
    text_piece = lax.all_gather(text_emb, "narrow", axis=0, tiled=True)
    image_piece = lax.all_gather(image_emb, "narrow", axis=0, tiled=True)
    partner_piece = lax.all_gather(partner_row, "narrow", axis=0, tiled=True)
    columns = jnp.arange(text_piece.shape[0], dtype=jnp.int32)
    pair_mine = pair_terms(image_emb, text_piece, partner_row[:, None] == columns[None, :])
    pair_other = pair_terms(image_piece, text_emb, partner_piece[:, None] == my_columns[None, :])
    image_grad = jnp.dot(pair_mine, text_piece, preferred_element_type=jnp.float32)
    text_grad = lax.dot_general(
        pair_other, image_piece, (((0,), (0,)), ((), ())), preferred_element_type=jnp.float32
    )
    image_grad, text_grad = (image_grad, text_grad)
    image_pg = proj_backward(image_proj, image_inv, image_grad)
    text_pg = proj_backward(text_proj, text_inv, text_grad)
    image_feature_grad = lax.dot_general(
        image_pg, image_weight, (((1,), (1,)), ((), ())), preferred_element_type=jnp.float32
    ).astype(jnp.bfloat16)
    text_feature_grad = lax.dot_general(
        text_pg, text_weight, (((1,), (1,)), ((), ())), preferred_element_type=jnp.float32
    ).astype(jnp.bfloat16)
    image_term = lax.dot_general(
        image_features, image_pg, (((0,), (0,)), ((), ())), preferred_element_type=jnp.float32
    )
    text_term = lax.dot_general(
        text_features, text_pg, (((0,), (0,)), ((), ())), preferred_element_type=jnp.float32
    )
    rows_part = (
        lax.psum_scatter(image_term, "wide", scatter_dimension=0, tiled=True),
        lax.psum_scatter(text_term, "wide", scatter_dimension=0, tiled=True),
    )
    image_weight_grad, text_weight_grad = (
        lax.psum_scatter(rows_part[0], "narrow", scatter_dimension=1, tiled=True),
        lax.psum_scatter(rows_part[1], "narrow", scatter_dimension=1, tiled=True),
    )
    return (image_feature_grad, text_feature_grad, image_weight_grad, text_weight_grad)


def solution(mesh):
    in_specs = (
        P(("wide", "narrow"), None),
        P(("wide", "narrow"), None),
        P(),
        P(),
        P("wide", "narrow"),
    )
    out_specs = (
        P(("wide", "narrow"), None),
        P(("wide", "narrow"), None),
        P("wide", "narrow"),
        P("wide", "narrow"),
    )
    return jax.shard_map(local, mesh=mesh, in_specs=in_specs, out_specs=out_specs, check_vma=False)
```

profile of v0, /device:TPU:2, one launch (start us, length us, event | category | flops | bytes accessed | tf_op | source)
XLA Modules:
  0.0 876.8 jit_solution(11903444437595785252)
XLA Ops:
  7.2 0.0 copy-start
  7.2 0.0 copy-start.3
  7.2 0.0 all-gather.6.cloned.1.call-start
  7.2 2.9 multiply_reduce_fusion.3
  10.2 0.0 copy-start.1
  10.2 0.9 copy-done.1
  11.1 0.9 multiply_convert_fusion.1
  12.0 0.0 all-gather.6.cloned.1.call-update
  12.0 0.0 copy-start.7
  12.0 0.0 copy-start.4
  12.0 0.0 all-gather.4.cloned.1.call-start
  12.1 0.0 copy-done
  12.1 0.0 copy-done.3
  12.1 0.9 multiply_reduce_fusion.2
  13.0 0.0 copy-start.2
  13.0 0.9 copy-done.2
  13.9 0.9 multiply_convert_fusion
  14.8 0.0 all-gather.4.cloned.1.call-update
  14.8 0.0 all-reduce.6.cloned.1.call-start
  14.9 0.0 copy-done.7
  14.9 0.6 dynamic-slice
  16.2 0.2 dynamic-update-slice
  16.4 5.0 all-reduce
  21.4 22.6 %all-gather.6.cloned.1.call-done = bf16[768,1152]{1,0:T(8,128)(2,1)} async-done(((bf16[192,1152]{1,0:T(8,128)(2,1)}), bf16[768,1152]{1,0:T(8,128)(2,1)}) %all-gather.6.cloned.1.call-update) | async-done | bytes 1769488 | tf_op jit(solution)/shard_map/all_gather | solution.py:39
  44.0 6.0 multiply_reduce_fusion
  50.0 1.6 subtract_convert_fusion
  51.6 0.0 copy-start.5
  51.7 3.3 convolution_bitcast_fusion
  55.0 21.3 %all-gather.4.cloned.1.call-done = bf16[768,1152]{1,0:T(8,128)(2,1)} async-done(((bf16[192,1152]{1,0:T(8,128)(2,1)}), bf16[768,1152]{1,0:T(8,128)(2,1)}) %all-gather.4.cloned.1.call-update) | async-done | bytes 1769488 | tf_op jit(solution)/shard_map/all_gather | solution.py:38
  76.3 5.0 multiply_reduce_fusion.1
  81.3 1.6 subtract_convert_fusion.1
  83.0 4.3 convolution_bitcast_fusion.1
  87.2 0.0 all-reduce.6.cloned.1.call-update
  87.3 0.0 reduce-scatter.5.cloned.1.call-start
  87.3 0.6 copy-done.6
  87.9 0.6 dynamic-slice.1
  89.2 1.8 convolution_convert_fusion
  90.9 703.1 %all-reduce.6.cloned.1.call-done = (f32[1152,1152]{0,1:T(8,128)}, f32[1152,1152]{0,1:T(8,128)}) async-done(((f32[1152,1152]{0,1:T(8,128)}, f32[1152,1152]{0,1:T(8,128)}), (f32[1152,1152]{0,1:T(8,128)}, f32[1152,1152]{0,1:T(8,128)})) %all-reduce.6.cloned.1.call-update) | async-done | bytes 10616848
  794.1 2.3 constant_dynamic-slice_fusion.1
  796.4 0.0 reduce-scatter.5.cloned.1.call-update
  796.4 0.0 reduce-scatter.7.cloned.1.call-start
  796.4 2.3 constant_dynamic-slice_fusion
  798.8 0.0 reduce-scatter.7.cloned.1.call-update
  798.8 3.5 convolution_convert_fusion.1
  802.3 41.8 %reduce-scatter.5.cloned.1.call-done = f32[18,288]{0,1:T(8,128)} async-done(((f32[18,1152]{0,1:T(8,128)}), f32[18,288]{0,1:T(8,128)}) %reduce-scatter.5.cloned.1.call-update) | async-done | bytes 20752 | tf_op jit(solution)/shard_map/reduce_scatter | solution.py:68
  844.2 1.6 copy.11
  845.8 22.9 %reduce-scatter.7.cloned.1.call-done = f32[18,288]{0,1:T(8,128)} async-done(((f32[18,1152]{0,1:T(8,128)}), f32[18,288]{0,1:T(8,128)}) %reduce-scatter.7.cloned.1.call-update) | async-done | bytes 20752 | tf_op jit(solution)/shard_map/reduce_scatter | solution.py:69
  868.7 1.6 copy.12
  (7 shorter events, 0.0 us)
Async XLA Ops:
  7.2 4.9 copy-start
  7.2 4.9 copy-start.3
  7.2 36.8 %all-gather.6.cloned.1.call-start = ((), (), s32[]{:S(2)}) async-start(), calls=%async_computation.3 | async-start | bytes 2211840 | tf_op jit(solution)/shard_map/all_gather | solution.py:39
  10.2 0.9 copy-start.1
  12.0 2.9 copy-start.7
  12.0 4.1 copy-start.4
  12.0 64.3 %all-gather.4.cloned.1.call-start = ((), (), s32[]{:S(2)}) async-start(), calls=%async_computation.2 | async-start | bytes 2211840 | tf_op jit(solution)/shard_map/all_gather | solution.py:38
  13.0 0.9 copy-start.2
  14.8 779.2 %all-reduce.6.cloned.1.call-start = ((), (), s32[]{:S(2)}) async-start(), calls=%async_computation.6 | async-start | bytes 21233664
  51.6 24.7 %copy-start.5 = (s32[1,192]{1,0:T(1,128)S(1)}, s32[1,192]{1,0:T(1,128)}, u32[]{:S(2)}) copy-start(s32[1,192]{1,0:T(1,128)} %param.9) | copy-start | bytes 2308
  87.2 0.7 copy-start.6
  87.3 756.9 %reduce-scatter.5.cloned.1.call-start = ((), (), s32[]{:S(2)}) async-start(), calls=%async_computation.4 | async-start | bytes 737280 | tf_op jit(solution)/shard_map/reduce_scatter | solution.py:68
  796.4 72.3 %reduce-scatter.7.cloned.1.call-start = ((), (), s32[]{:S(2)}) async-start(), calls=%async_computation.5 | async-start | bytes 737280 | tf_op jit(solution)/shard_map/reduce_scatter | solution.py:69
Sparse Core Ops, SparseCore 0:
  12.1 31.8 all-gather.5
  46.4 29.8 all-gather.3
  87.4 706.6 all-reduce.5
  796.6 47.5 reduce-scatter.4
  846.7 21.9 reduce-scatter.6
where the time goes:
time: 879 us; the launch traced here: 877 us
  waiting for transfers between devices  812 us (92%)
  matrix products  27.8 us (3%)
  between operations  15.2 us (2%)
  local copies, waits for them, and re-layouts  11.8 us (1%)
    unnamed x6, waiting for transfers between devices  703 us
    reduce_scatter x1, waiting for transfers between devices, local(): lax.psum_scatter(rows_part[0], 'narrow', scatter_dimension=1, tiled=True)  41.8 us
    reduce_scatter x1, waiting for transfers between devices, local(): lax.psum_scatter(rows_part[1], 'narrow', scatter_dimension=1, tiled=True)  22.9 us
    all_gather x1, waiting for transfers between devices, local(): image_piece = lax.all_gather(image_emb, 'narrow', axis=0, tiled=True)  22.6 us
    all_gather x1, waiting for transfers between devices, local(): text_piece = lax.all_gather(text_emb, 'narrow', axis=0, tiled=True)  21.3 us
  transfers between devices with their start and end apart: 5, of which 5 were waited for; matrix products, arithmetic and copies ran while one was open for 3% of the time, Pallas kernels for 0%

commit v1 on v0

v1 whole, which is shorter than its diff:
```python
import functools

import jax
import jax.numpy as jnp
from jax import lax
from jax.experimental import pallas as pl
from jax.experimental.pallas import tpu as pltpu
from jax.sharding import PartitionSpec as P

logit_scale = 10.0
logit_bias = -2.0
norm_eps = 1e-06

NX, NYH = 4, 2
PIECES = 2
WINDOW = 640
CORE_STEP = 512
PART = 384
PART_STEP = 256
PAD = 32

OWN_CORE, OWN_CHIP, FORWARD = 0, PIECES, 2 * PIECES
CORE_SUM = 3 * PIECES
X_RELAY, X_DIRECT, X_BOTH = CORE_SUM + 4, CORE_SUM + 6, CORE_SUM + 8
Y_SUM = CORE_SUM + 10
Z_SUM = Y_SUM + 3


def kernel(nz, f_i, f_t, w_i_hbm, w_t_hbm, partner, fg_i, fg_t, wg_i, wg_t,
           w, ft, proj, inv, grad, emb, pairs, pg, pgp,
           core_out, core_in, relay_out, relay_in, direct_out, direct_in, both_out, both_in, keep, acc,
           y_out, y_in, z_out, z_in, w_sem, p_send, p_recv, send, recv):
    rows, depth = f_i.shape
    width = w.shape[2]
    chunk = depth // NX
    half = chunk // NYH
    mine = half // nz
    quarter = width // 4
    features = (f_i, f_t)
    wide, narrow = lax.axis_index("wide"), lax.axis_index("narrow")
    z, yh, x = lax.rem(wide, nz), lax.rem(wide // nz, NYH), wide // (nz * NYH)
    yl, c = narrow // 2, lax.rem(narrow, 2)

    def device(x=x, yh=yh, z=z, yl=yl, c=c):
        return ((x * NYH + yh) * nz + z, yl * 2 + c)

    core_peer = device(c=1 - c)
    chip_peer = device(yl=1 - yl)
    far_peer = device(yl=1 - yl, c=1 - c)
    block_core, block_chip, block_far = yl * 2 + 1 - c, (1 - yl) * 2 + c, (1 - yl) * 2 + 1 - c
    x_next, x_prev, x_far = lax.rem(x + 1, NX), lax.rem(x + NX - 1, NX), lax.rem(x + 2, NX)
    next_peer, prev_peer = device(x=x_next), device(x=x_prev)
    y_peers = (
        (yh, 1 - yl, device(yh=yh, yl=1 - yl)),
        (1 - yh, yl, device(yh=1 - yh, yl=yl)),
        (1 - yh, 1 - yl, device(yh=1 - yh, yl=1 - yl)),
    )
    z_peers = [(lax.rem(z + d, nz), device(z=lax.rem(z + d, nz))) for d in range(1, nz)]

    loads = []
    for m, src in ((1, w_t_hbm), (0, w_i_hbm)):
        load = pltpu.make_async_copy(src, w.at[m], w_sem.at[m])
        load.start()
        loads.append(load)

    barrier = pltpu.get_barrier_semaphore()
    peers = [core_peer, chip_peer, far_peer, next_peer, prev_peer, y_peers[1][2], y_peers[2][2]]
    peers += [peer for _, peer in z_peers]
    for peer in peers:
        pl.semaphore_signal(barrier, inc=1, device_id=peer, device_id_type=pl.DeviceIdType.MESH)

    def remote(src, dst, m, s, peer):
        return pltpu.make_async_remote_copy(
            src_ref=src, dst_ref=dst, send_sem=send.at[m, s], recv_sem=recv.at[m, s],
            device_id=peer, device_id_type=pl.DeviceIdType.MESH)

    started = []

    def go(copy):
        copy.start()
        started.append(copy)
        return copy

    piece = rows // PIECES
    own = {}

    def embed(m):
        p = jnp.dot(features[m][...], w[m], preferred_element_type=jnp.float32)
        i = lax.rsqrt(jnp.sum(p * p, axis=1, keepdims=True) + norm_eps)
        proj[m] = p
        inv[m] = i
        emb[m, narrow] = (p * i).astype(jnp.bfloat16)

    def send_own(m):
        for k in range(PIECES):
            ref = emb.at[m, narrow, pl.ds(k * piece, piece)]
            own[m, 0, k] = go(remote(ref, ref, m, OWN_CORE + k, core_peer))
            own[m, 1, k] = go(remote(ref, ref, m, OWN_CHIP + k, chip_peer))

    def forward(m):
        for k in range(PIECES):
            own[m, 1, k].wait_recv()
            ref = emb.at[m, block_chip, pl.ds(k * piece, piece)]
            own[m, 2, k] = go(remote(ref, ref, m, FORWARD + k, core_peer))

    def arrived(m, kind):
        for k in range(PIECES):
            own[m, kind, k].wait_recv()

    loads[0].wait()
    embed(1)
    pl.semaphore_wait(barrier, len(peers))
    send_own(1)
    pairs[narrow] = partner[...]
    pair_copies = []
    for s, peer in enumerate((core_peer, chip_peer, far_peer)):
        copy = pltpu.make_async_remote_copy(
            src_ref=pairs.at[narrow], dst_ref=pairs.at[narrow], send_sem=p_send.at[s], recv_sem=p_recv.at[s],
            device_id=peer, device_id_type=pl.DeviceIdType.MESH)
        pair_copies.append(go(copy))
    loads[1].wait()
    embed(0)
    send_own(0)

    for m in (0, 1):
        ft[m] = features[m][...].T

    down = lax.broadcasted_iota(jnp.int32, (rows, rows), 0)
    along = lax.broadcasted_iota(jnp.int32, (rows, rows), 1)
    partner_down = jnp.sum(
        jnp.where(down == along, partner[...].astype(jnp.float32), 0.0), axis=1, keepdims=True
    ).astype(jnp.int32)

    def add_block(m, block, first):
        other = emb[1 - m, block]
        logits = logit_scale * lax.dot_general(
            emb[m, narrow], other, (((1,), (1,)), ((), ())), preferred_element_type=jnp.float32
        ) + logit_bias
        if m == 0:
            match = partner_down == block * rows + along
        else:
            match = pairs[block] == narrow * rows + down
        pair = jnp.where(match, -logit_scale, logit_scale) * jax.nn.sigmoid(jnp.where(match, -logits, logits))
        part = jnp.dot(pair.astype(jnp.bfloat16), other, preferred_element_type=jnp.float32)
        grad[m] = part if first else grad[m] + part

    def project_back(m):
        p, i, g = proj[m], inv[m], grad[m]
        total = jnp.sum(p * g, axis=1, keepdims=True)
        value = i * g - p * (i * i * i * total)
        pg[m] = value.astype(jnp.bfloat16)
        q = quarter
        moved = jnp.concatenate([value[:, :q], value[:, 2 * q:3 * q], value[:, q:2 * q], value[:, 3 * q:]], axis=1)
        pgp[m] = moved.astype(jnp.bfloat16)

    def feature_grad(m, out):
        out[...] = lax.dot_general(
            pg[m], w[m], (((1,), (1,)), ((), ())), preferred_element_type=jnp.float32
        ).astype(jnp.bfloat16)

    targets = (x_far, x_next, x_prev, x)

    def share(m, xd, core):
        left = ft[m, pl.ds(pl.multiple_of(xd * chunk, 16), chunk), :]
        right = pgp[m, :, pl.ds(pl.multiple_of(core * CORE_STEP, 128), WINDOW)]
        return jnp.dot(left, right, preferred_element_type=jnp.float32)

    core_copies, x_copies, y_copies, z_copies = {}, {}, {}, {}

    def core_start(m):
        for k, xd in enumerate(targets):
            core_out[m, k] = share(m, xd, 1 - c).astype(jnp.bfloat16)
            core_copies[m, k] = go(remote(core_out.at[m, k], core_in.at[m, k], m, CORE_SUM + k, core_peer))

    def chip_share(m, k):
        total = share(m, targets[k], c)
        core_copies[m, k].wait_recv()
        return total + core_in[m, k].astype(jnp.float32)

    def x_send(m, s, out, into, t, peer):
        x_copies[m, s + t] = go(remote(out.at[m, t], into.at[m, t], m, s + t, peer))

    def x_start(m):
        total = chip_share(m, 0)
        for t, peer in enumerate((next_peer, prev_peer)):
            relay_out[m, t] = total[t * half:(t + 1) * half].astype(jnp.bfloat16)
            x_send(m, X_RELAY, relay_out, relay_in, t, peer)
        for t, peer in enumerate((next_peer, prev_peer)):
            total = chip_share(m, 1 + t)
            direct_out[m, t] = total[(1 - t) * half:(2 - t) * half].astype(jnp.bfloat16)
            x_send(m, X_DIRECT, direct_out, direct_in, t, peer)
            keep[m, t] = total[t * half:(t + 1) * half]
        acc[m] = chip_share(m, 3)

    def x_relay(m):
        for t, peer in enumerate((next_peer, prev_peer)):
            x_copies[m, X_RELAY + t].wait_recv()
            both_out[m, t] = (keep[m, t] + relay_in[m, t].astype(jnp.float32)).astype(jnp.bfloat16)
            x_send(m, X_BOTH, both_out, both_in, t, peer)

    def x_finish(m):
        for t in range(2):
            x_copies[m, X_DIRECT + t].wait_recv()
            acc[m, (1 - t) * half:(2 - t) * half] += direct_in[m, t].astype(jnp.float32)
        for t in range(2):
            x_copies[m, X_BOTH + t].wait_recv()
            acc[m, t * half:(t + 1) * half] += both_in[m, t].astype(jnp.float32)

    def y_part(m, h, l):
        return acc[m, pl.ds(pl.multiple_of(h * half, 16), half), pl.ds(pl.multiple_of(l * PART_STEP, 128), PART)]

    def y_start(m):
        for s, (h, l, peer) in enumerate(y_peers):
            y_out[m, s] = y_part(m, h, l).astype(jnp.bfloat16)
            y_copies[m, s] = go(remote(y_out.at[m, s], y_in.at[m, s], m, Y_SUM + s, peer))

    def z_start(m):
        total = y_part(m, yh, yl)
        for s in range(3):
            y_copies[m, s].wait_recv()
            total = total + y_in[m, s].astype(jnp.float32)
        row = lax.broadcasted_iota(jnp.int32, (nz * PAD, half), 0)
        column = lax.broadcasted_iota(jnp.int32, (nz * PAD, half), 1)
        which, within = row // PAD, lax.rem(row, PAD)
        spread = jnp.where((within < mine) & (column == which * mine + within), 1.0, 0.0).astype(jnp.bfloat16)
        padded = jnp.dot(spread, total.astype(jnp.bfloat16), preferred_element_type=jnp.float32).astype(jnp.bfloat16)
        for d in range(nz):
            z_out[m, d] = padded[d * PAD:(d + 1) * PAD]
        for s, (zd, peer) in enumerate(z_peers):
            z_copies[m, s] = go(remote(z_out.at[m, zd], z_in.at[m, s], m, Z_SUM + s, peer))

    def z_finish(m, out):
        total = z_out[m, z].astype(jnp.float32)
        for s in range(nz - 1):
            z_copies[m, s].wait_recv()
            total = total + z_in[m, s].astype(jnp.float32)
        shift = lax.rem(PART - (quarter - PART_STEP) * (yl + 2 * c), PART)
        out[...] = pltpu.roll(total, shift, 1)[:mine, :quarter]

    add = add_block
    add(0, narrow, True)
    pair_copies[0].wait_recv()
    add(1, narrow, True)
    arrived(1, 0)
    add(0, block_core, False)
    arrived(0, 0)
    add(1, block_core, False)

    forward(1)
    add(0, block_chip, False)
    arrived(1, 2)
    add(0, block_far, False)
    project_back(0)
    core_start(0)
    x_start(0)
    feature_grad(0, fg_i)

    forward(0)
    pair_copies[1].wait_recv()
    pair_copies[2].wait_recv()
    add(1, block_chip, False)
    arrived(0, 2)
    add(1, block_far, False)
    project_back(1)
    core_start(1)
    x_relay(0)
    x_start(1)
    x_finish(0)
    y_start(0)
    feature_grad(1, fg_t)
    x_relay(1)
    z_start(0)
    x_finish(1)
    y_start(1)
    z_finish(0, wg_i)
    z_start(1)
    z_finish(1, wg_t)
    for copy in started:
        copy.wait_send()


def local(nz, image_features, text_features, image_weight, text_weight, partner):
    rows, depth = image_features.shape
    width = image_weight.shape[1]
    chunk = depth // NX
    half = chunk // NYH
    mine = half // nz
    b16, f32 = jnp.bfloat16, jnp.float32
    vmem = pl.BlockSpec(memory_space=pltpu.VMEM)
    hbm = pl.BlockSpec(memory_space=pl.ANY)
    copies = Z_SUM + max(nz - 1, 1)
    return pl.pallas_call(
        functools.partial(kernel, nz),
        out_shape=(
            jax.ShapeDtypeStruct((rows, depth), b16),
            jax.ShapeDtypeStruct((rows, depth), b16),
            jax.ShapeDtypeStruct((mine, width // 4), f32),
            jax.ShapeDtypeStruct((mine, width // 4), f32),
        ),
        in_specs=[vmem, vmem, hbm, hbm, vmem],
        out_specs=(vmem,) * 4,
        scratch_shapes=[
            pltpu.VMEM((2, depth, width), b16),
            pltpu.VMEM((2, depth, rows), b16),
            pltpu.VMEM((2, rows, width), f32),
            pltpu.VMEM((2, rows, 1), f32),
            pltpu.VMEM((2, rows, width), f32),
            pltpu.VMEM((2, 4, rows, width), b16),
            pltpu.VMEM((4, 1, rows), jnp.int32),
            pltpu.VMEM((2, rows, width), b16),
            pltpu.VMEM((2, rows, width), b16),
            pltpu.VMEM((2, 4, chunk, WINDOW), b16),
            pltpu.VMEM((2, 4, chunk, WINDOW), b16),
            pltpu.VMEM((2, 2, half, WINDOW), b16),
            pltpu.VMEM((2, 2, half, WINDOW), b16),
            pltpu.VMEM((2, 2, half, WINDOW), b16),
            pltpu.VMEM((2, 2, half, WINDOW), b16),
            pltpu.VMEM((2, 2, half, WINDOW), b16),
            pltpu.VMEM((2, 2, half, WINDOW), b16),
            pltpu.VMEM((2, 2, half, WINDOW), f32),
            pltpu.VMEM((2, chunk, WINDOW), f32),
            pltpu.VMEM((2, 3, half, PART), b16),
            pltpu.VMEM((2, 3, half, PART), b16),
            pltpu.VMEM((2, nz, PAD, PART), b16),
            pltpu.VMEM((2, max(nz - 1, 1), PAD, PART), b16),
            pltpu.SemaphoreType.DMA((2,)),
            pltpu.SemaphoreType.DMA((3,)),
            pltpu.SemaphoreType.DMA((3,)),
            pltpu.SemaphoreType.DMA((2, copies)),
            pltpu.SemaphoreType.DMA((2, copies)),
        ],
        compiler_params=pltpu.CompilerParams(
            collective_id=0, has_side_effects=True, vmem_limit_bytes=56 * 1024 * 1024),
        cost_estimate=pl.CostEstimate(flops=4_500_000_000, bytes_accessed=8_000_000, transcendentals=300_000),
    )(image_features, text_features, image_weight, text_weight, partner)


def solution(mesh):
    in_specs = (
        P(("wide", "narrow"), None),
        P(("wide", "narrow"), None),
        P(),
        P(),
        P("wide", "narrow"),
    )
    out_specs = (
        P(("wide", "narrow"), None),
        P(("wide", "narrow"), None),
        P("wide", "narrow"),
        P("wide", "narrow"),
    )
    nz = mesh.shape["wide"] // (NX * NYH)
    return jax.shard_map(
        functools.partial(local, nz), mesh=mesh, in_specs=in_specs, out_specs=out_specs, check_vma=False)
```

time: 879 us -> 77.7 us (0.09)
  the two profiles are of different devices: /device:TPU:2 before, /device:TPU:1 now
where the time goes in v1:
time: 77.7 us; the launch traced here: 77.3 us
  Pallas kernels  70.3 us (90%)
  local copies, waits for them, and re-layouts  6.39 us (8%)
    pallas_call x1, Pallas kernels, local(): pl.pallas_call(functools.partial(kernel, nz), out_shape=(jax.ShapeDtypeSt...  70.3 us
    unnamed x4, local copies, waits for them, and re-layouts  6.39 us

profile of v1, /device:TPU:1, one launch (start us, length us, event | category | flops | bytes accessed | tf_op | source)
XLA Modules:
  0.0 77.3 jit_solution(13883931876117332857)
XLA Ops:
  0.6 70.3 %shard_map.84 = (bf16[192,1152]{1,0:T(8,128)(2,1)}, bf16[192,1152]{1,0:T(8,128)(2,1)}, f32[18,288]{1,0:T(8,128)}, f32[18,288]{1,0:T(8,128)}) custom-call(bf16[192,1152]{1,0:T(8,128)(2,1)} %f_i.1, bf16[192,1152]{1,0:T(8,128)(2,1)} %f_t.1, bf16[1152,1152]{1,0:T(8,128)(2,1)} %w_i_hbm.1, bf16[1152,1152]{1,0:T(8,128)(2,1)} %w_t_hbm.1, s32[1,192]{1,0:T(1,128)} %partner.1), custom_call_target="tpu_custom_call" | custom-call | flops 4499999744 | bytes 8000000 | tf_op jit(solution)/shard_map/pallas_call | solution.py:292
  70.9 1.8 %copy.13 = bf16[192,1152]{1,0:T(8,128)(2,1)} copy(bf16[192,1152]{1,0:T(8,128)(2,1)} %get-tuple-element.8) | data formatting | bytes 884736
  72.8 1.8 %copy.14 = bf16[192,1152]{1,0:T(8,128)(2,1)} copy(bf16[192,1152]{1,0:T(8,128)(2,1)} %get-tuple-element.9) | data formatting | bytes 884736
  74.6 1.4 %copy.15 = f32[18,288]{1,0:T(8,128)} copy(f32[18,288]{1,0:T(8,128)} %get-tuple-element.10) | data formatting | bytes 41472
  75.9 1.4 %copy.16 = f32[18,288]{1,0:T(8,128)} copy(f32[18,288]{1,0:T(8,128)} %get-tuple-element.11) | data formatting | bytes 41472

commit v2 on v1

--- a/solution.py
+++ b/solution.py
@@ -17,19 +17,19 @@
 CORE_STEP = 512
 PART = 384
 PART_STEP = 256
-PAD = 32
+TILE = 16
+Y_FIRST = 64
 
 OWN_CORE, OWN_CHIP, FORWARD = 0, PIECES, 2 * PIECES
 CORE_SUM = 3 * PIECES
-X_RELAY, X_DIRECT, X_BOTH = CORE_SUM + 4, CORE_SUM + 6, CORE_SUM + 8
-Y_SUM = CORE_SUM + 10
-Z_SUM = Y_SUM + 3
+Z_SUM = CORE_SUM + 4
+RINGS = 6
 
 
 def kernel(nz, f_i, f_t, w_i_hbm, w_t_hbm, partner, fg_i, fg_t, wg_i, wg_t,
            w, ft, proj, inv, grad, emb, pairs, pg, pgp,
-           core_out, core_in, relay_out, relay_in, direct_out, direct_in, both_out, both_in, keep, acc,
-           y_out, y_in, z_out, z_in, w_sem, p_send, p_recv, send, recv):
+           core_out, core_in, acc, sums_i, sums_t, sums_y, last, z_out, z_in, ring_bufs,
+           w_sem, p_send, p_recv, send, recv, ring_send, ring_recv):
     rows, depth = f_i.shape
     width = w.shape[2]
     chunk = depth // NX
@@ -49,12 +49,12 @@
     far_peer = device(yl=1 - yl, c=1 - c)
     block_core, block_chip, block_far = yl * 2 + 1 - c, (1 - yl) * 2 + c, (1 - yl) * 2 + 1 - c
     x_next, x_prev, x_far = lax.rem(x + 1, NX), lax.rem(x + NX - 1, NX), lax.rem(x + 2, NX)
-    next_peer, prev_peer = device(x=x_next), device(x=x_prev)
-    y_peers = (
-        (yh, 1 - yl, device(yh=yh, yl=1 - yl)),
-        (1 - yh, yl, device(yh=1 - yh, yl=yl)),
-        (1 - yh, 1 - yl, device(yh=1 - yh, yl=1 - yl)),
-    )
+    y = yh * 2 + yl
+    y_far, y_next, y_prev = lax.rem(y + 2, 4), lax.rem(y + 1, 4), lax.rem(y + 3, 4)
+    x_targets = (x_far, x_next, x_prev, x)
+    y_targets = (y_far, y_next, y_prev, y)
+    x_pair = (device(x=x_next), device(x=x_prev))
+    y_pair = tuple(device(yh=t // 2, yl=lax.rem(t, 2)) for t in (y_next, y_prev))
     z_peers = [(lax.rem(z + d, nz), device(z=lax.rem(z + d, nz))) for d in range(1, nz)]
 
     loads = []
@@ -64,7 +64,7 @@
         loads.append(load)
 
     barrier = pltpu.get_barrier_semaphore()
-    peers = [core_peer, chip_peer, far_peer, next_peer, prev_peer, y_peers[1][2], y_peers[2][2]]
+    peers = [core_peer, chip_peer, far_peer, *x_pair, device(yh=1 - yh, yl=1 - yl)]
     peers += [peer for _, peer in z_peers]
     for peer in peers:
         pl.semaphore_signal(barrier, inc=1, device_id=peer, device_id_type=pl.DeviceIdType.MESH)
@@ -158,74 +158,114 @@
             pg[m], w[m], (((1,), (1,)), ((), ())), preferred_element_type=jnp.float32
         ).astype(jnp.bfloat16)
 
-    targets = (x_far, x_next, x_prev, x)
-
     def share(m, xd, core):
         left = ft[m, pl.ds(pl.multiple_of(xd * chunk, 16), chunk), :]
         right = pgp[m, :, pl.ds(pl.multiple_of(core * CORE_STEP, 128), WINDOW)]
         return jnp.dot(left, right, preferred_element_type=jnp.float32)
 
-    core_copies, x_copies, y_copies, z_copies = {}, {}, {}, {}
+    core_copies, z_copies = {}, {}
 
     def core_start(m):
-        for k, xd in enumerate(targets):
+        for k, xd in enumerate(x_targets):
             core_out[m, k] = share(m, xd, 1 - c).astype(jnp.bfloat16)
             core_copies[m, k] = go(remote(core_out.at[m, k], core_in.at[m, k], m, CORE_SUM + k, core_peer))
 
     def chip_share(m, k):
-        total = share(m, targets[k], c)
+        total = share(m, x_targets[k], c)
         core_copies[m, k].wait_recv()
-        return total + core_in[m, k].astype(jnp.float32)
-
-    def x_send(m, s, out, into, t, peer):
-        x_copies[m, s + t] = go(remote(out.at[m, t], into.at[m, t], m, s + t, peer))
-
-    def x_start(m):
-        total = chip_share(m, 0)
-        for t, peer in enumerate((next_peer, prev_peer)):
-            relay_out[m, t] = total[t * half:(t + 1) * half].astype(jnp.bfloat16)
-            x_send(m, X_RELAY, relay_out, relay_in, t, peer)
-        for t, peer in enumerate((next_peer, prev_peer)):
-            total = chip_share(m, 1 + t)
-            direct_out[m, t] = total[(1 - t) * half:(2 - t) * half].astype(jnp.bfloat16)
-            x_send(m, X_DIRECT, direct_out, direct_in, t, peer)
-            keep[m, t] = total[t * half:(t + 1) * half]
-        acc[m] = chip_share(m, 3)
-
-    def x_relay(m):
-        for t, peer in enumerate((next_peer, prev_peer)):
-            x_copies[m, X_RELAY + t].wait_recv()
-            both_out[m, t] = (keep[m, t] + relay_in[m, t].astype(jnp.float32)).astype(jnp.bfloat16)
-            x_send(m, X_BOTH, both_out, both_in, t, peer)
-
-    def x_finish(m):
-        for t in range(2):
-            x_copies[m, X_DIRECT + t].wait_recv()
-            acc[m, (1 - t) * half:(2 - t) * half] += direct_in[m, t].astype(jnp.float32)
-        for t in range(2):
-            x_copies[m, X_BOTH + t].wait_recv()
-            acc[m, t * half:(t + 1) * half] += both_in[m, t].astype(jnp.float32)
-
-    def y_part(m, h, l):
-        return acc[m, pl.ds(pl.multiple_of(h * half, 16), half), pl.ds(pl.multiple_of(l * PART_STEP, 128), PART)]
-
-    def y_start(m):
-        for s, (h, l, peer) in enumerate(y_peers):
-            y_out[m, s] = y_part(m, h, l).astype(jnp.bfloat16)
-            y_copies[m, s] = go(remote(y_out.at[m, s], y_in.at[m, s], m, Y_SUM + s, peer))
+        acc[m, k] = total + core_in[m, k].astype(jnp.float32)
+
+    class Ring:
+        def __init__(self, n, pair, value):
+            self.n, self.pair, self.value, self.copies = n, pair, value, {}
+
+        def push(self, h, kind, peer, value):
+            out, into = ring_bufs[self.n][h]
+            out[kind] = value.astype(jnp.bfloat16)
+            s = h * 3 + kind
+            self.copies[h, kind] = go(pltpu.make_async_remote_copy(
+                src_ref=out.at[kind], dst_ref=into.at[kind],
+                send_sem=ring_send.at[self.n, s], recv_sem=ring_recv.at[self.n, s],
+                device_id=peer, device_id_type=pl.DeviceIdType.MESH))
+
+        def pull(self, h, kind):
+            self.copies[h, kind].wait_recv()
+            return ring_bufs[self.n][h][1][kind].astype(jnp.float32)
+
+        def relay(self, h):
+            self.push(h, 0, self.pair[h], self.value(0, h))
+
+        def direct(self, h):
+            self.push(h, 1, self.pair[1 - h], self.value(2 - h, h))
+
+        def both(self):
+            for h in range(2):
+                self.push(h, 2, self.pair[h], self.value(1 + h, h) + self.pull(h, 0))
+
+        def total(self, h):
+            return self.value(3, h) + self.pull(h, 1) + self.pull(h, 2)
+
+    def x_first(m, low):
+        return lambda k, h: acc[m, k, h * half + low:(h + 1) * half, :]
+
+    def column_part(l):
+        return pl.ds(pl.multiple_of(l * PART_STEP, 128), PART)
+
+    def y_second(sums, cuts):
+        def value(k, h):
+            t = y_targets[k]
+            return sums[t // 2, cuts[h]:cuts[h + 1], column_part(lax.rem(t, 2))]
+        return value
+
+    def y_first(k, h):
+        t = y_targets[k]
+        block = pl.ds(pl.multiple_of((t // 2) * half, 8), Y_FIRST)
+        return acc[1, 2 * h:2 * h + 2, block, column_part(lax.rem(t, 2))]
+
+    def x_second(k, h):
+        n = Y_FIRST // 2
+        return sums_y[k, h * n:(h + 1) * n, :]
+
+    cuts_i, cuts_t = (0, 80, half), (0, 48, half - Y_FIRST)
+    ring_ix = Ring(0, x_pair, x_first(0, 0))
+    ring_iy = Ring(1, y_pair, y_second(sums_i, cuts_i))
+    ring_tx = Ring(2, x_pair, x_first(1, Y_FIRST))
+    ring_txy = Ring(3, y_pair, y_second(sums_t, cuts_t))
+    ring_ty = Ring(4, y_pair, y_first)
+    ring_tyx = Ring(5, x_pair, x_second)
+
+    def begin(ring):
+        ring.relay(0)
+        ring.relay(1)
+        ring.direct(1)
+        ring.direct(0)
+
+    spare = PART - quarter
+    segments = quarter // spare
+    rest = mine - TILE
 
     def z_start(m):
-        total = y_part(m, yh, yl)
-        for s in range(3):
-            y_copies[m, s].wait_recv()
-            total = total + y_in[m, s].astype(jnp.float32)
-        row = lax.broadcasted_iota(jnp.int32, (nz * PAD, half), 0)
-        column = lax.broadcasted_iota(jnp.int32, (nz * PAD, half), 1)
-        which, within = row // PAD, lax.rem(row, PAD)
-        spread = jnp.where((within < mine) & (column == which * mine + within), 1.0, 0.0).astype(jnp.bfloat16)
-        padded = jnp.dot(spread, total.astype(jnp.bfloat16), preferred_element_type=jnp.float32).astype(jnp.bfloat16)
+        total = last[m]
+        offset = (quarter - PART_STEP) * (yl + 2 * c)
+        total = pltpu.roll(total, lax.rem(PART - offset, PART), 1)
+        row = lax.broadcasted_iota(jnp.int32, (nz * TILE, half), 0)
+        column = lax.broadcasted_iota(jnp.int32, (nz * TILE, half), 1)
+        which, within = row // TILE, lax.rem(row, TILE)
+
+        def pick(chosen, source, value):
+            spread = jnp.where(chosen & (column == which * mine + source), 1.0, 0.0).astype(jnp.bfloat16)
+            return jnp.dot(spread, value.astype(jnp.bfloat16), preferred_element_type=jnp.float32)
+
+        body = pick(within < TILE, within, total)
+        tail = jnp.zeros_like(body)
+        for s in range(segments):
+            moved = pltpu.roll(total, quarter - s * spare, 1)
+            chosen = (within < rest * segments) & (lax.rem(within, segments) == s)
+            tail = tail + pick(chosen, TILE + within // segments, moved)
+        lane = lax.broadcasted_iota(jnp.int32, body.shape, 1)
+        packed = jnp.where(lane < quarter, body, tail).astype(jnp.bfloat16)
         for d in range(nz):
-            z_out[m, d] = padded[d * PAD:(d + 1) * PAD]
+            z_out[m, d] = packed[d * TILE:(d + 1) * TILE]
         for s, (zd, peer) in enumerate(z_peers):
             z_copies[m, s] = go(remote(z_out.at[m, zd], z_in.at[m, s], m, Z_SUM + s, peer))
 
@@ -234,8 +274,10 @@
         for s in range(nz - 1):
             z_copies[m, s].wait_recv()
             total = total + z_in[m, s].astype(jnp.float32)
-        shift = lax.rem(PART - (quarter - PART_STEP) * (yl + 2 * c), PART)
-        out[...] = pltpu.roll(total, shift, 1)[:mine, :quarter]
+        out[:TILE, :] = total[:, :quarter]
+        for r in range(rest):
+            rows_of = [total[r * segments + s:r * segments + s + 1, quarter:] for s in range(segments)]
+            out[TILE + r:TILE + r + 1, :] = jnp.concatenate(rows_of, axis=1)
 
     add = add_block
     add(0, narrow, True)
@@ -252,7 +294,14 @@
     add(0, block_far, False)
     project_back(0)
     core_start(0)
-    x_start(0)
+    chip_share(0, 0)
+    ring_ix.relay(0)
+    ring_ix.relay(1)
+    chip_share(0, 1)
+    ring_ix.direct(1)
+    chip_share(0, 2)
+    ring_ix.direct(0)
+    chip_share(0, 3)
     feature_grad(0, fg_i)
 
     forward(0)
@@ -263,20 +312,52 @@
     add(1, block_far, False)
     project_back(1)
     core_start(1)
-    x_relay(0)
-    x_start(1)
-    x_finish(0)
-    y_start(0)
+    ring_ix.both()
+    chip_share(1, 0)
+    ring_tx.relay(0)
+    ring_tx.relay(1)
+    chip_share(1, 1)
+    ring_ty.relay(0)
+    ring_ty.direct(0)
+    ring_tx.direct(1)
+    chip_share(1, 2)
+    ring_tx.direct(0)
+    chip_share(1, 3)
+    ring_ty.relay(1)
+    ring_ty.direct(1)
+
+    for h in range(2):
+        sums_i[h] = ring_ix.total(h)
+    begin(ring_iy)
+    ring_tx.both()
+    ring_ty.both()
+    ring_iy.both()
     feature_grad(1, fg_t)
-    x_relay(1)
+    for h in range(2):
+        sums_t[h] = ring_tx.total(h)
+    begin(ring_txy)
+    for h in range(2):
+        sums_y[2 * h:2 * h + 2] = ring_ty.total(h)
+    begin(ring_tyx)
+    for h in range(2):
+        last[0, cuts_i[h]:cuts_i[h + 1]] = ring_iy.total(h)
     z_start(0)
-    x_finish(1)
-    y_start(1)
+    ring_txy.both()
+    ring_tyx.both()
+    for h in range(2):
+        n = Y_FIRST // 2
+        last[1, h * n:(h + 1) * n] = ring_tyx.total(h)
+    for h in range(2):
+        last[1, Y_FIRST + cuts_t[h]:Y_FIRST + cuts_t[h + 1]] = ring_txy.total(h)
+    z_start(1)
     z_finish(0, wg_i)
-    z_start(1)
     z_finish(1, wg_t)
     for copy in started:
         copy.wait_send()
+
+
+def hand_over(a, b, c, d, a_out, b_out, c_out, d_out):
+    a_out[...], b_out[...], c_out[...], d_out[...] = a[...], b[...], c[...], d[...]
 
 
 def local(nz, image_features, text_features, image_weight, text_weight, partner):
@@ -288,8 +369,18 @@
     b16, f32 = jnp.bfloat16, jnp.float32
     vmem = pl.BlockSpec(memory_space=pltpu.VMEM)
     hbm = pl.BlockSpec(memory_space=pl.ANY)
-    copies = Z_SUM + max(nz - 1, 1)
-    return pl.pallas_call(
+    copies = Z_SUM + nz - 1
+    rest = half - Y_FIRST
+    ring_shapes = [
+        ((half, WINDOW), (half, WINDOW)),
+        ((80, PART), (half - 80, PART)),
+        ((rest, WINDOW), (rest, WINDOW)),
+        ((48, PART), (rest - 48, PART)),
+        ((2, Y_FIRST, PART), (2, Y_FIRST, PART)),
+        ((Y_FIRST // 2, PART), (Y_FIRST // 2, PART)),
+    ]
+    rings = [[[pltpu.VMEM((3, *shape), b16) for _ in range(2)] for shape in pair] for pair in ring_shapes]
+    outs = pl.pallas_call(
         functools.partial(kernel, nz),
         out_shape=(
             jax.ShapeDtypeStruct((rows, depth), b16),
@@ -311,28 +402,32 @@
             pltpu.VMEM((2, rows, width), b16),
             pltpu.VMEM((2, 4, chunk, WINDOW), b16),
             pltpu.VMEM((2, 4, chunk, WINDOW), b16),
-            pltpu.VMEM((2, 2, half, WINDOW), b16),
-            pltpu.VMEM((2, 2, half, WINDOW), b16),
-            pltpu.VMEM((2, 2, half, WINDOW), b16),
-            pltpu.VMEM((2, 2, half, WINDOW), b16),
-            pltpu.VMEM((2, 2, half, WINDOW), b16),
-            pltpu.VMEM((2, 2, half, WINDOW), b16),
-            pltpu.VMEM((2, 2, half, WINDOW), f32),
-            pltpu.VMEM((2, chunk, WINDOW), f32),
-            pltpu.VMEM((2, 3, half, PART), b16),
-            pltpu.VMEM((2, 3, half, PART), b16),
-            pltpu.VMEM((2, nz, PAD, PART), b16),
-            pltpu.VMEM((2, max(nz - 1, 1), PAD, PART), b16),
+            pltpu.VMEM((2, 4, chunk, WINDOW), f32),
+            pltpu.VMEM((2, half, WINDOW), f32),
+            pltpu.VMEM((2, rest, WINDOW), f32),
+            pltpu.VMEM((4, Y_FIRST, PART), f32),
+            pltpu.VMEM((2, half, PART), f32),
+            pltpu.VMEM((2, nz, TILE, PART), b16),
+            pltpu.VMEM((2, nz - 1, TILE, PART), b16),
+            rings,
             pltpu.SemaphoreType.DMA((2,)),
             pltpu.SemaphoreType.DMA((3,)),
             pltpu.SemaphoreType.DMA((3,)),
             pltpu.SemaphoreType.DMA((2, copies)),
             pltpu.SemaphoreType.DMA((2, copies)),
+            pltpu.SemaphoreType.DMA((RINGS, 6)),
+            pltpu.SemaphoreType.DMA((RINGS, 6)),
         ],
         compiler_params=pltpu.CompilerParams(
             collective_id=0, has_side_effects=True, vmem_limit_bytes=56 * 1024 * 1024),
         cost_estimate=pl.CostEstimate(flops=4_500_000_000, bytes_accessed=8_000_000, transcendentals=300_000),
     )(image_features, text_features, image_weight, text_weight, partner)
+    return pl.pallas_call(
+        hand_over,
+        out_shape=[jax.ShapeDtypeStruct(out.shape, out.dtype) for out in outs],
+        in_specs=[vmem] * 4,
+        out_specs=[vmem] * 4,
+    )(*outs)
 
 
 def solution(mesh):

time: 77.7 us -> 65.4 us (0.84)
  the two profiles are of different devices: /device:TPU:1 before, /device:TPU:2 now
where the time goes in v2:
time: 65.4 us; the launch traced here: 65.2 us
  Pallas kernels  64.6 us (99%)
    pallas_call x1, Pallas kernels, local(): pl.pallas_call(functools.partial(kernel, nz), out_shape=(jax.ShapeDtypeSt...  62.5 us
    pallas_call x1, Pallas kernels, local(): pl.pallas_call(hand_over, out_shape=[jax.ShapeDtypeStruct(out.shape, out....  2.11 us

profile of v2, /device:TPU:2, one launch (start us, length us, event | category | flops | bytes accessed | tf_op | source)
XLA Modules:
  0.0 65.2 jit_solution(15792021700223962586)
XLA Ops:
  0.6 62.5 %shard_map.84 = (bf16[192,1152]{1,0:T(8,128)(2,1)}, bf16[192,1152]{1,0:T(8,128)(2,1)}, f32[18,288]{1,0:T(8,128)}, f32[18,288]{1,0:T(8,128)}) custom-call(bf16[192,1152]{1,0:T(8,128)(2,1)} %f_i.1, bf16[192,1152]{1,0:T(8,128)(2,1)} %f_t.1, bf16[1152,1152]{1,0:T(8,128)(2,1)} %w_i_hbm.1, bf16[1152,1152]{1,0:T(8,128)(2,1)} %w_t_hbm.1, s32[1,192]{1,0:T(1,128)} %partner.1), custom_call_target="tpu_custom_call" | custom-call | flops 4499999744 | bytes 8000000 | tf_op jit(solution)/shard_map/pallas_call | solution.py:383
  63.1 2.1 %shard_map.85 = (bf16[192,1152]{1,0:T(8,128)(2,1)}, bf16[192,1152]{1,0:T(8,128)(2,1)}, f32[18,288]{1,0:T(8,128)}, f32[18,288]{1,0:T(8,128)}) custom-call(bf16[192,1152]{1,0:T(8,128)(2,1)} %get-tuple-element.8.a, bf16[192,1152]{1,0:T(8,128)(2,1)} %get-tuple-element.9.b, f32[18,288]{1,0:T(8,128)} %get-tuple-element.10.c, f32[18,288]{1,0:T(8,128)} %get-tuple-element.11.d), custom_call_target="tpu_custom_call" | custom-call | tf_op jit(solution)/shard_map/pallas_call | solution.py:425

commit v3 on v2

--- a/solution.py
+++ b/solution.py
@@ -18,18 +18,23 @@
 PART = 384
 PART_STEP = 256
 TILE = 16
+PAD = 32
+CUT = 80
 Y_FIRST = 64
 
 OWN_CORE, OWN_CHIP, FORWARD = 0, PIECES, 2 * PIECES
 CORE_SUM = 3 * PIECES
-Z_SUM = CORE_SUM + 4
+Z_SUM = CORE_SUM + 8
 RINGS = 6
 
 
+Z_ORDER = (4, 3, -3, 2, -2, 1, -1, 0)
+
+
 def kernel(nz, f_i, f_t, w_i_hbm, w_t_hbm, partner, fg_i, fg_t, wg_i, wg_t,
-           w, ft, proj, inv, grad, emb, pairs, pg, pgp,
-           core_out, core_in, acc, sums_i, sums_t, sums_y, last, z_out, z_in, ring_bufs,
-           w_sem, p_send, p_recv, send, recv, ring_send, ring_recv):
+           w, ft, ft_z, proj, inv, grad, emb, pairs, pg, pgp,
+           out_i, in_i, out_t, in_t, acc_i, acc, sums_i, sums_ix, sums_t, sums_y, last_i, last, z_out, z_in,
+           long_bufs, ring_bufs, w_sem, p_send, p_recv, send, recv, long_send, long_recv, ring_send, ring_recv):
     rows, depth = f_i.shape
     width = w.shape[2]
     chunk = depth // NX
@@ -97,11 +102,10 @@
             own[m, 0, k] = go(remote(ref, ref, m, OWN_CORE + k, core_peer))
             own[m, 1, k] = go(remote(ref, ref, m, OWN_CHIP + k, chip_peer))
 
-    def forward(m):
-        for k in range(PIECES):
-            own[m, 1, k].wait_recv()
-            ref = emb.at[m, block_chip, pl.ds(k * piece, piece)]
-            own[m, 2, k] = go(remote(ref, ref, m, FORWARD + k, core_peer))
+    def forward(m, k):
+        own[m, 1, k].wait_recv()
+        ref = emb.at[m, block_chip, pl.ds(k * piece, piece)]
+        own[m, 2, k] = go(remote(ref, ref, m, FORWARD + k, core_peer))
 
     def arrived(m, kind):
         for k in range(PIECES):
@@ -122,8 +126,15 @@
     embed(0)
     send_own(0)
 
-    for m in (0, 1):
-        ft[m] = features[m][...].T
+    ft[...] = f_t[...].T
+    row = lax.broadcasted_iota(jnp.int32, (half, 1), 0)
+    source = (row // mine) * half + lax.rem(row, mine)
+    column = lax.broadcasted_iota(jnp.int32, (half, depth), 1)
+    for d in range(nz):
+        order = jnp.where(column == source + d * mine, 1.0, 0.0).astype(jnp.bfloat16)
+        ft_z[d] = lax.dot_general(
+            order, f_i[...], (((1,), (1,)), ((), ())), preferred_element_type=jnp.float32
+        ).astype(jnp.bfloat16)
 
     down = lax.broadcasted_iota(jnp.int32, (rows, rows), 0)
     along = lax.broadcasted_iota(jnp.int32, (rows, rows), 1)
@@ -158,22 +169,72 @@
             pg[m], w[m], (((1,), (1,)), ((), ())), preferred_element_type=jnp.float32
         ).astype(jnp.bfloat16)
 
-    def share(m, xd, core):
-        left = ft[m, pl.ds(pl.multiple_of(xd * chunk, 16), chunk), :]
+    def share(left, m, core):
         right = pgp[m, :, pl.ds(pl.multiple_of(core * CORE_STEP, 128), WINDOW)]
         return jnp.dot(left, right, preferred_element_type=jnp.float32)
 
+    def rows_of(m, k):
+        if m == 0:
+            return ft_z[lax.rem(z + Z_ORDER[k] + nz, nz)]
+        return ft[pl.ds(pl.multiple_of(x_targets[k] * chunk, 16), chunk), :]
+
     core_copies, z_copies = {}, {}
-
-    def core_start(m):
-        for k, xd in enumerate(x_targets):
-            core_out[m, k] = share(m, xd, 1 - c).astype(jnp.bfloat16)
-            core_copies[m, k] = go(remote(core_out.at[m, k], core_in.at[m, k], m, CORE_SUM + k, core_peer))
+    core_bufs = ((out_i, in_i, acc_i), (out_t, in_t, acc))
+
+    def core_start(m, k):
+        out, into, _ = core_bufs[m]
+        out[k] = share(rows_of(m, k), m, 1 - c).astype(jnp.bfloat16)
+        core_copies[m, k] = go(remote(out.at[k], into.at[k], m, CORE_SUM + k, core_peer))
 
     def chip_share(m, k):
-        total = share(m, x_targets[k], c)
+        _, into, total = core_bufs[m]
+        part = share(rows_of(m, k), m, c)
         core_copies[m, k].wait_recv()
-        acc[m, k] = total + core_in[m, k].astype(jnp.float32)
+        total[k] = part + into[k].astype(jnp.float32)
+
+    z_pair = (device(z=lax.rem(z + 1, nz)), device(z=lax.rem(z + nz - 1, nz)))
+    spans = (pl.ds(0, CUT), pl.ds(CUT, half - CUT))
+    long_copies = {}
+
+    def own_part(d, h):
+        return acc_i[Z_ORDER.index(d), spans[h], :]
+
+    def long_push(way, hops, far):
+        h = way if far else 1 - way
+        out, into = long_bufs[way][h]
+        value = own_part(hops if way == 0 or hops == nz // 2 else -hops, h)
+        first = nz // 2 if far else nz // 2 - 1
+        if hops < first:
+            value = value + long_pull(way, hops + 1, far)
+        slot = first - hops
+        out[slot] = value.astype(jnp.bfloat16)
+        s = 2 * slot + (0 if far else 1)
+        long_copies[way, hops, far] = go(pltpu.make_async_remote_copy(
+            src_ref=out.at[slot], dst_ref=into.at[slot], send_sem=long_send.at[way, s], recv_sem=long_recv.at[way, s],
+            device_id=z_pair[way], device_id_type=pl.DeviceIdType.MESH))
+
+    def long_pull(way, hops, far):
+        long_copies[way, hops, far].wait_recv()
+        h = way if far else 1 - way
+        first = nz // 2 if far else nz // 2 - 1
+        return long_bufs[way][h][1][first - hops].astype(jnp.float32)
+
+    def long_step(hops, far):
+        for way in range(2):
+            long_push(way, hops, far)
+
+    def spread_rows():
+        low = own_part(0, 0) + long_pull(0, 1, True) + long_pull(1, 1, False)
+        high = own_part(0, 1) + long_pull(0, 1, False) + long_pull(1, 1, True)
+        row = lax.broadcasted_iota(jnp.int32, (8 * PAD, 1), 0)
+        within = lax.rem(row, PAD)
+        source = jnp.where(within < mine, (row // PAD) * mine + within, -1)
+        column = lax.broadcasted_iota(jnp.int32, (8 * PAD, half), 1)
+        spread = jnp.where(column == source, 1.0, 0.0).astype(jnp.bfloat16)
+        total = jnp.concatenate([low, high], axis=0).astype(jnp.bfloat16)
+        total = jnp.dot(spread, total, preferred_element_type=jnp.float32)
+        for d in range(8):
+            sums_i[d] = total[d * PAD:(d + 1) * PAD]
 
     class Ring:
         def __init__(self, n, pair, value):
@@ -205,8 +266,11 @@
         def total(self, h):
             return self.value(3, h) + self.pull(h, 1) + self.pull(h, 2)
 
-    def x_first(m, low):
-        return lambda k, h: acc[m, k, h * half + low:(h + 1) * half, :]
+    def x_first(k, h):
+        return acc[k, h * half + Y_FIRST:(h + 1) * half, :]
+
+    def x_after_z(k, h):
+        return sums_i[x_targets[k] * NYH + h]
 
     def column_part(l):
         return pl.ds(pl.multiple_of(l * PART_STEP, 128), PART)
@@ -220,16 +284,16 @@
     def y_first(k, h):
         t = y_targets[k]
         block = pl.ds(pl.multiple_of((t // 2) * half, 8), Y_FIRST)
-        return acc[1, 2 * h:2 * h + 2, block, column_part(lax.rem(t, 2))]
+        return acc[2 * h:2 * h + 2, block, column_part(lax.rem(t, 2))]
 
     def x_second(k, h):
         n = Y_FIRST // 2
         return sums_y[k, h * n:(h + 1) * n, :]
 
-    cuts_i, cuts_t = (0, 80, half), (0, 48, half - Y_FIRST)
-    ring_ix = Ring(0, x_pair, x_first(0, 0))
-    ring_iy = Ring(1, y_pair, y_second(sums_i, cuts_i))
-    ring_tx = Ring(2, x_pair, x_first(1, Y_FIRST))
+    cuts_i, cuts_t = (0, PAD // 2, PAD), (0, 48, half - Y_FIRST)
+    ring_ix = Ring(0, x_pair, x_after_z)
+    ring_iy = Ring(1, y_pair, y_second(sums_ix, cuts_i))
+    ring_tx = Ring(2, x_pair, x_first)
     ring_txy = Ring(3, y_pair, y_second(sums_t, cuts_t))
     ring_ty = Ring(4, y_pair, y_first)
     ring_tyx = Ring(5, x_pair, x_second)
@@ -244,10 +308,12 @@
     segments = quarter // spare
     rest = mine - TILE
 
-    def z_start(m):
-        total = last[m]
+    def to_left(value):
         offset = (quarter - PART_STEP) * (yl + 2 * c)
-        total = pltpu.roll(total, lax.rem(PART - offset, PART), 1)
+        return pltpu.roll(value, lax.rem(PART - offset, PART), 1)
+
+    def z_start():
+        total = to_left(last[...])
         row = lax.broadcasted_iota(jnp.int32, (nz * TILE, half), 0)
         column = lax.broadcasted_iota(jnp.int32, (nz * TILE, half), 1)
         which, within = row // TILE, lax.rem(row, TILE)
@@ -265,19 +331,19 @@
         lane = lax.broadcasted_iota(jnp.int32, body.shape, 1)
         packed = jnp.where(lane < quarter, body, tail).astype(jnp.bfloat16)
         for d in range(nz):
-            z_out[m, d] = packed[d * TILE:(d + 1) * TILE]
+            z_out[d] = packed[d * TILE:(d + 1) * TILE]
         for s, (zd, peer) in enumerate(z_peers):
-            z_copies[m, s] = go(remote(z_out.at[m, zd], z_in.at[m, s], m, Z_SUM + s, peer))
-
-    def z_finish(m, out):
-        total = z_out[m, z].astype(jnp.float32)
+            z_copies[s] = go(remote(z_out.at[zd], z_in.at[s], 1, Z_SUM + s, peer))
+
+    def z_finish(out):
+        total = z_out[z].astype(jnp.float32)
         for s in range(nz - 1):
-            z_copies[m, s].wait_recv()
-            total = total + z_in[m, s].astype(jnp.float32)
+            z_copies[s].wait_recv()
+            total = total + z_in[s].astype(jnp.float32)
         out[:TILE, :] = total[:, :quarter]
         for r in range(rest):
-            rows_of = [total[r * segments + s:r * segments + s + 1, quarter:] for s in range(segments)]
-            out[TILE + r:TILE + r + 1, :] = jnp.concatenate(rows_of, axis=1)
+            pieces = [total[r * segments + s:r * segments + s + 1, quarter:] for s in range(segments)]
+            out[TILE + r:TILE + r + 1, :] = jnp.concatenate(pieces, axis=1)
 
     add = add_block
     add(0, narrow, True)
@@ -288,34 +354,43 @@
     arrived(0, 0)
     add(1, block_core, False)
 
-    forward(1)
+    forward(1, 0)
+    forward(1, 1)
     add(0, block_chip, False)
     arrived(1, 2)
     add(0, block_far, False)
     project_back(0)
-    core_start(0)
-    chip_share(0, 0)
-    ring_ix.relay(0)
-    ring_ix.relay(1)
-    chip_share(0, 1)
-    ring_ix.direct(1)
-    chip_share(0, 2)
-    ring_ix.direct(0)
-    chip_share(0, 3)
+    half_z = nz // 2
+    ahead = 3
+    for k in range(nz + ahead):
+        if k < nz:
+            core_start(0, k)
+        if k == ahead:
+            chip_share(0, 0)
+            long_step(half_z, True)
+        elif k == ahead + 1 or k == ahead + 2:
+            chip_share(0, k - ahead)
+            long_push(k - ahead - 1, half_z - 1, False)
+        elif k > ahead:
+            chip_share(0, k - ahead)
+    forward(0, 0)
     feature_grad(0, fg_i)
-
-    forward(0)
+    long_step(3, True)
+
+    forward(0, 1)
     pair_copies[1].wait_recv()
     pair_copies[2].wait_recv()
     add(1, block_chip, False)
     arrived(0, 2)
     add(1, block_far, False)
     project_back(1)
-    core_start(1)
-    ring_ix.both()
+    core_start(1, 0)
+    core_start(1, 1)
+    core_start(1, 2)
     chip_share(1, 0)
     ring_tx.relay(0)
     ring_tx.relay(1)
+    core_start(1, 3)
     chip_share(1, 1)
     ring_ty.relay(0)
     ring_ty.direct(0)
@@ -325,13 +400,13 @@
     chip_share(1, 3)
     ring_ty.relay(1)
     ring_ty.direct(1)
-
-    for h in range(2):
-        sums_i[h] = ring_ix.total(h)
-    begin(ring_iy)
+    long_step(2, False)
+    long_step(2, True)
+
     ring_tx.both()
     ring_ty.both()
-    ring_iy.both()
+    long_step(1, False)
+    long_step(1, True)
     feature_grad(1, fg_t)
     for h in range(2):
         sums_t[h] = ring_tx.total(h)
@@ -339,19 +414,25 @@
     for h in range(2):
         sums_y[2 * h:2 * h + 2] = ring_ty.total(h)
     begin(ring_tyx)
-    for h in range(2):
-        last[0, cuts_i[h]:cuts_i[h + 1]] = ring_iy.total(h)
-    z_start(0)
+    spread_rows()
+    begin(ring_ix)
     ring_txy.both()
     ring_tyx.both()
+    ring_ix.both()
     for h in range(2):
         n = Y_FIRST // 2
-        last[1, h * n:(h + 1) * n] = ring_tyx.total(h)
+        last[h * n:(h + 1) * n] = ring_tyx.total(h)
     for h in range(2):
-        last[1, Y_FIRST + cuts_t[h]:Y_FIRST + cuts_t[h + 1]] = ring_txy.total(h)
-    z_start(1)
-    z_finish(0, wg_i)
-    z_finish(1, wg_t)
+        last[Y_FIRST + cuts_t[h]:Y_FIRST + cuts_t[h + 1]] = ring_txy.total(h)
+    z_start()
+    for h in range(2):
+        sums_ix[h] = ring_ix.total(h)
+    begin(ring_iy)
+    ring_iy.both()
+    for h in range(2):
+        last_i[cuts_i[h]:cuts_i[h + 1]] = ring_iy.total(h)
+    wg_i[...] = to_left(last_i[...])[:mine, :quarter]
+    z_finish(wg_t)
     for copy in started:
         copy.wait_send()
 
@@ -372,14 +453,19 @@
     copies = Z_SUM + nz - 1
     rest = half - Y_FIRST
     ring_shapes = [
-        ((half, WINDOW), (half, WINDOW)),
-        ((80, PART), (half - 80, PART)),
+        ((PAD, WINDOW), (PAD, WINDOW)),
+        ((PAD // 2, PART), (PAD // 2, PART)),
         ((rest, WINDOW), (rest, WINDOW)),
         ((48, PART), (rest - 48, PART)),
         ((2, Y_FIRST, PART), (2, Y_FIRST, PART)),
         ((Y_FIRST // 2, PART), (Y_FIRST // 2, PART)),
     ]
     rings = [[[pltpu.VMEM((3, *shape), b16) for _ in range(2)] for shape in pair] for pair in ring_shapes]
+    long_rows, hops = (CUT, half - CUT), nz // 2
+    longs = [
+        [[pltpu.VMEM((hops if h == way else hops - 1, long_rows[h], WINDOW), b16) for _ in range(2)] for h in range(2)]
+        for way in range(2)
+    ]
     outs = pl.pallas_call(
         functools.partial(kernel, nz),
         out_shape=(
@@ -392,7 +478,8 @@
         out_specs=(vmem,) * 4,
         scratch_shapes=[
             pltpu.VMEM((2, depth, width), b16),
-            pltpu.VMEM((2, depth, rows), b16),
+            pltpu.VMEM((depth, rows), b16),
+            pltpu.VMEM((nz, half, rows), b16),
             pltpu.VMEM((2, rows, width), f32),
             pltpu.VMEM((2, rows, 1), f32),
             pltpu.VMEM((2, rows, width), f32),
@@ -400,21 +487,29 @@
             pltpu.VMEM((4, 1, rows), jnp.int32),
             pltpu.VMEM((2, rows, width), b16),
             pltpu.VMEM((2, rows, width), b16),
-            pltpu.VMEM((2, 4, chunk, WINDOW), b16),
-            pltpu.VMEM((2, 4, chunk, WINDOW), b16),
-            pltpu.VMEM((2, 4, chunk, WINDOW), f32),
-            pltpu.VMEM((2, half, WINDOW), f32),
+            pltpu.VMEM((nz, half, WINDOW), b16),
+            pltpu.VMEM((nz, half, WINDOW), b16),
+            pltpu.VMEM((4, chunk, WINDOW), b16),
+            pltpu.VMEM((4, chunk, WINDOW), b16),
+            pltpu.VMEM((nz, half, WINDOW), f32),
+            pltpu.VMEM((4, chunk, WINDOW), f32),
+            pltpu.VMEM((8, PAD, WINDOW), f32),
+            pltpu.VMEM((2, PAD, WINDOW), f32),
             pltpu.VMEM((2, rest, WINDOW), f32),
             pltpu.VMEM((4, Y_FIRST, PART), f32),
-            pltpu.VMEM((2, half, PART), f32),
-            pltpu.VMEM((2, nz, TILE, PART), b16),
-            pltpu.VMEM((2, nz - 1, TILE, PART), b16),
+            pltpu.VMEM((PAD, PART), f32),
+            pltpu.VMEM((half, PART), f32),
+            pltpu.VMEM((nz, TILE, PART), b16),
+            pltpu.VMEM((nz - 1, TILE, PART), b16),
+            longs,
             rings,
             pltpu.SemaphoreType.DMA((2,)),
             pltpu.SemaphoreType.DMA((3,)),
             pltpu.SemaphoreType.DMA((3,)),
             pltpu.SemaphoreType.DMA((2, copies)),
             pltpu.SemaphoreType.DMA((2, copies)),
+            pltpu.SemaphoreType.DMA((2, 7)),
+            pltpu.SemaphoreType.DMA((2, 7)),
             pltpu.SemaphoreType.DMA((RINGS, 6)),
             pltpu.SemaphoreType.DMA((RINGS, 6)),
         ],

time: 65.4 us -> 67.5 us (1.032)
  Pallas kernels: 64.6 us -> 66.7 us
    pallas_call x1, Pallas kernels: 62.5 us -> 64.6 us  [local(): pl.pallas_call(functools.partial(kernel, nz), out_shape=(jax.ShapeDtypeSt...]
where the time goes in v3:
time: 67.5 us; the launch traced here: 67.4 us
  Pallas kernels  66.7 us (99%)
    pallas_call x1, Pallas kernels, local(): pl.pallas_call(functools.partial(kernel, nz), out_shape=(jax.ShapeDtypeSt...  64.6 us
    pallas_call x1, Pallas kernels, local(): pl.pallas_call(hand_over, out_shape=[jax.ShapeDtypeStruct(out.shape, out....  2.11 us

profile of v3, /device:TPU:2, one launch (start us, length us, event | category | flops | bytes accessed | tf_op | source)
XLA Modules:
  0.0 67.4 jit_solution(2015693850939844772)
XLA Ops:
  0.6 64.6 %shard_map.84 = (bf16[192,1152]{1,0:T(8,128)(2,1)}, bf16[192,1152]{1,0:T(8,128)(2,1)}, f32[18,288]{1,0:T(8,128)}, f32[18,288]{1,0:T(8,128)}) custom-call(bf16[192,1152]{1,0:T(8,128)(2,1)} %f_i.1, bf16[192,1152]{1,0:T(8,128)(2,1)} %f_t.1, bf16[1152,1152]{1,0:T(8,128)(2,1)} %w_i_hbm.1, bf16[1152,1152]{1,0:T(8,128)(2,1)} %w_t_hbm.1, s32[1,192]{1,0:T(1,128)} %partner.1), custom_call_target="tpu_custom_call" | custom-call | flops 4499999744 | bytes 8000000 | tf_op jit(solution)/shard_map/pallas_call | solution.py:469
  65.3 2.1 %shard_map.85 = (bf16[192,1152]{1,0:T(8,128)(2,1)}, bf16[192,1152]{1,0:T(8,128)(2,1)}, f32[18,288]{1,0:T(8,128)}, f32[18,288]{1,0:T(8,128)}) custom-call(bf16[192,1152]{1,0:T(8,128)(2,1)} %get-tuple-element.8.a, bf16[192,1152]{1,0:T(8,128)(2,1)} %get-tuple-element.9.b, f32[18,288]{1,0:T(8,128)} %get-tuple-element.10.c, f32[18,288]{1,0:T(8,128)} %get-tuple-element.11.d), custom_call_target="tpu_custom_call" | custom-call | tf_op jit(solution)/shard_map/pallas_call | solution.py:520

commit v4 on v2

--- a/solution.py
+++ b/solution.py
@@ -26,10 +26,10 @@
 RINGS = 6
 
 
-def kernel(nz, f_i, f_t, w_i_hbm, w_t_hbm, partner, fg_i, fg_t, wg_i, wg_t,
-           w, ft, proj, inv, grad, emb, pairs, pg, pgp,
+def kernel(nz, f_i_hbm, f_t_hbm, w_i_hbm, w_t_hbm, partner_hbm, fg_i_hbm, fg_t_hbm, wg_i, wg_t,
+           f_i, f_t, partner, fg, fg_sem, w, ft, proj, inv, grad, emb, pairs, pg, pgp,
            core_out, core_in, acc, sums_i, sums_t, sums_y, last, z_out, z_in, ring_bufs,
-           w_sem, p_send, p_recv, send, recv, ring_send, ring_recv):
+           f_sem, w_sem, p_send, p_recv, send, recv, ring_send, ring_recv):
     rows, depth = f_i.shape
     width = w.shape[2]
     chunk = depth // NX
@@ -57,17 +57,22 @@
     y_pair = tuple(device(yh=t // 2, yl=lax.rem(t, 2)) for t in (y_next, y_prev))
     z_peers = [(lax.rem(z + d, nz), device(z=lax.rem(z + d, nz))) for d in range(1, nz)]
 
-    loads = []
-    for m, src in ((1, w_t_hbm), (0, w_i_hbm)):
-        load = pltpu.make_async_copy(src, w.at[m], w_sem.at[m])
-        load.start()
-        loads.append(load)
-
     barrier = pltpu.get_barrier_semaphore()
     peers = [core_peer, chip_peer, far_peer, *x_pair, device(yh=1 - yh, yl=1 - yl)]
     peers += [peer for _, peer in z_peers]
     for peer in peers:
         pl.semaphore_signal(barrier, inc=1, device_id=peer, device_id_type=pl.DeviceIdType.MESH)
+
+    loads = []
+    sources = ((f_t_hbm, f_t), (f_i_hbm, f_i), (partner_hbm, partner))
+    feature_loads = [pltpu.make_async_copy(src, dst, f_sem.at[k]) for k, (src, dst) in enumerate(sources)]
+    feature_loads[0].start()
+    for m, src in ((1, w_t_hbm), (0, w_i_hbm)):
+        load = pltpu.make_async_copy(src, w.at[m], w_sem.at[m])
+        load.start()
+        loads.append(load)
+    feature_loads[1].start()
+    feature_loads[2].start()
 
     def remote(src, dst, m, s, peer):
         return pltpu.make_async_remote_copy(
@@ -107,10 +112,12 @@
         for k in range(PIECES):
             own[m, kind, k].wait_recv()
 
+    feature_loads[0].wait()
     loads[0].wait()
     embed(1)
     pl.semaphore_wait(barrier, len(peers))
     send_own(1)
+    feature_loads[2].wait()
     pairs[narrow] = partner[...]
     pair_copies = []
     for s, peer in enumerate((core_peer, chip_peer, far_peer)):
@@ -118,6 +125,7 @@
             src_ref=pairs.at[narrow], dst_ref=pairs.at[narrow], send_sem=p_send.at[s], recv_sem=p_recv.at[s],
             device_id=peer, device_id_type=pl.DeviceIdType.MESH)
         pair_copies.append(go(copy))
+    feature_loads[1].wait()
     loads[1].wait()
     embed(0)
     send_own(0)
@@ -148,15 +156,20 @@
         p, i, g = proj[m], inv[m], grad[m]
         total = jnp.sum(p * g, axis=1, keepdims=True)
         value = i * g - p * (i * i * i * total)
-        pg[m] = value.astype(jnp.bfloat16)
+        value = value.astype(jnp.bfloat16)
+        pg[m] = value
         q = quarter
-        moved = jnp.concatenate([value[:, :q], value[:, 2 * q:3 * q], value[:, q:2 * q], value[:, 3 * q:]], axis=1)
-        pgp[m] = moved.astype(jnp.bfloat16)
+        pgp[m] = jnp.concatenate([value[:, :q], value[:, 2 * q:3 * q], value[:, q:2 * q], value[:, 3 * q:]], axis=1)
+
+    fg_copies = []
 
     def feature_grad(m, out):
-        out[...] = lax.dot_general(
+        fg[m] = lax.dot_general(
             pg[m], w[m], (((1,), (1,)), ((), ())), preferred_element_type=jnp.float32
         ).astype(jnp.bfloat16)
+        copy = pltpu.make_async_copy(fg.at[m], out, fg_sem.at[m])
+        copy.start()
+        fg_copies.append(copy)
 
     def share(m, xd, core):
         left = ft[m, pl.ds(pl.multiple_of(xd * chunk, 16), chunk), :]
@@ -165,10 +178,9 @@
 
     core_copies, z_copies = {}, {}
 
-    def core_start(m):
-        for k, xd in enumerate(x_targets):
-            core_out[m, k] = share(m, xd, 1 - c).astype(jnp.bfloat16)
-            core_copies[m, k] = go(remote(core_out.at[m, k], core_in.at[m, k], m, CORE_SUM + k, core_peer))
+    def core_start(m, k):
+        core_out[m, k] = share(m, x_targets[k], 1 - c).astype(jnp.bfloat16)
+        core_copies[m, k] = go(remote(core_out.at[m, k], core_in.at[m, k], m, CORE_SUM + k, core_peer))
 
     def chip_share(m, k):
         total = share(m, x_targets[k], c)
@@ -293,16 +305,19 @@
     arrived(1, 2)
     add(0, block_far, False)
     project_back(0)
-    core_start(0)
+    core_start(0, 0)
+    core_start(0, 1)
+    core_start(0, 2)
     chip_share(0, 0)
     ring_ix.relay(0)
     ring_ix.relay(1)
+    core_start(0, 3)
     chip_share(0, 1)
     ring_ix.direct(1)
     chip_share(0, 2)
     ring_ix.direct(0)
     chip_share(0, 3)
-    feature_grad(0, fg_i)
+    feature_grad(0, fg_i_hbm)
 
     forward(0)
     pair_copies[1].wait_recv()
@@ -311,11 +326,14 @@
     arrived(0, 2)
     add(1, block_far, False)
     project_back(1)
-    core_start(1)
+    core_start(1, 0)
+    core_start(1, 1)
+    core_start(1, 2)
     ring_ix.both()
     chip_share(1, 0)
     ring_tx.relay(0)
     ring_tx.relay(1)
+    core_start(1, 3)
     chip_share(1, 1)
     ring_ty.relay(0)
     ring_ty.direct(0)
@@ -332,7 +350,7 @@
     ring_tx.both()
     ring_ty.both()
     ring_iy.both()
-    feature_grad(1, fg_t)
+    feature_grad(1, fg_t_hbm)
     for h in range(2):
         sums_t[h] = ring_tx.total(h)
     begin(ring_txy)
@@ -352,6 +370,8 @@
     z_start(1)
     z_finish(0, wg_i)
     z_finish(1, wg_t)
+    for copy in fg_copies:
+        copy.wait()
     for copy in started:
         copy.wait_send()
 
@@ -388,9 +408,14 @@
             jax.ShapeDtypeStruct((mine, width // 4), f32),
             jax.ShapeDtypeStruct((mine, width // 4), f32),
         ),
-        in_specs=[vmem, vmem, hbm, hbm, vmem],
-        out_specs=(vmem,) * 4,
+        in_specs=[hbm] * 5,
+        out_specs=(hbm, hbm, vmem, vmem),
         scratch_shapes=[
+            pltpu.VMEM((rows, depth), b16),
+            pltpu.VMEM((rows, depth), b16),
+            pltpu.VMEM((1, rows), jnp.int32),
+            pltpu.VMEM((2, rows, depth), b16),
+            pltpu.SemaphoreType.DMA((2,)),
             pltpu.VMEM((2, depth, width), b16),
             pltpu.VMEM((2, depth, rows), b16),
             pltpu.VMEM((2, rows, width), f32),
@@ -410,6 +435,7 @@
             pltpu.VMEM((2, nz, TILE, PART), b16),
             pltpu.VMEM((2, nz - 1, TILE, PART), b16),
             rings,
+            pltpu.SemaphoreType.DMA((3,)),
             pltpu.SemaphoreType.DMA((2,)),
             pltpu.SemaphoreType.DMA((3,)),
             pltpu.SemaphoreType.DMA((3,)),

time: 65.4 us -> 63.9 us (0.977)
  Pallas kernels: 64.6 us -> 63.1 us
    pallas_call x1, Pallas kernels: 62.5 us -> 61 us  [local(): pl.pallas_call(functools.partial(kernel, nz), out_shape=(jax.ShapeDtypeSt...]
where the time goes in v4:
time: 63.9 us; the launch traced here: 63.8 us
  Pallas kernels  63.1 us (99%)
  between operations  0.64 us (1%)
    pallas_call x1, Pallas kernels, local(): pl.pallas_call(functools.partial(kernel, nz), out_shape=(jax.ShapeDtypeSt...  61 us
    pallas_call x1, Pallas kernels, local(): pl.pallas_call(hand_over, out_shape=[jax.ShapeDtypeStruct(out.shape, out....  2.11 us

profile of v4, /device:TPU:2, one launch (start us, length us, event | category | flops | bytes accessed | tf_op | source)
XLA Modules:
  0.0 63.8 jit_solution(9024138952231538126)
XLA Ops:
  0.6 61.0 %shard_map.84 = (bf16[192,1152]{1,0:T(8,128)(2,1)}, bf16[192,1152]{1,0:T(8,128)(2,1)}, f32[18,288]{1,0:T(8,128)}, f32[18,288]{1,0:T(8,128)}) custom-call(bf16[192,1152]{1,0:T(8,128)(2,1)} %f_i_hbm.1, bf16[192,1152]{1,0:T(8,128)(2,1)} %f_t_hbm.1, bf16[1152,1152]{1,0:T(8,128)(2,1)} %w_i_hbm.1, bf16[1152,1152]{1,0:T(8,128)(2,1)} %w_t_hbm.1, s32[1,192]{1,0:T(1,128)} %partner_hbm.1), custom_call_target="tpu_custom_call" | custom-call | flops 4499999744 | bytes 8000000 | tf_op jit(solution)/shard_map/pallas_call | solution.py:403
  61.7 2.1 %shard_map.85 = (bf16[192,1152]{1,0:T(8,128)(2,1)}, bf16[192,1152]{1,0:T(8,128)(2,1)}, f32[18,288]{1,0:T(8,128)}, f32[18,288]{1,0:T(8,128)}) custom-call(bf16[192,1152]{1,0:T(8,128)(2,1)} %get-tuple-element.8.a, bf16[192,1152]{1,0:T(8,128)(2,1)} %get-tuple-element.9.b, f32[18,288]{1,0:T(8,128)} %get-tuple-element.10.c, f32[18,288]{1,0:T(8,128)} %get-tuple-element.11.d), custom_call_target="tpu_custom_call" | custom-call | tf_op jit(solution)/shard_map/pallas_call | solution.py:451

commit v5 on v4

--- a/solution.py
+++ b/solution.py
@@ -22,13 +22,13 @@
 
 OWN_CORE, OWN_CHIP, FORWARD = 0, PIECES, 2 * PIECES
 CORE_SUM = 3 * PIECES
-Z_SUM = CORE_SUM + 4
+Z_SUM = CORE_SUM + 2
 RINGS = 6
 
 
 def kernel(nz, f_i_hbm, f_t_hbm, w_i_hbm, w_t_hbm, partner_hbm, fg_i_hbm, fg_t_hbm, wg_i, wg_t,
            f_i, f_t, partner, fg, fg_sem, w, ft, proj, inv, grad, emb, pairs, pg, pgp,
-           core_out, core_in, acc, sums_i, sums_t, sums_y, last, z_out, z_in, ring_bufs,
+           f_peer, ft_peer, pg_peer, acc, sums_i, sums_t, sums_y, last, z_out, z_in, ring_bufs,
            f_sem, w_sem, p_send, p_recv, send, recv, ring_send, ring_recv):
     rows, depth = f_i.shape
     width = w.shape[2]
@@ -129,9 +129,13 @@
     loads[1].wait()
     embed(0)
     send_own(0)
+    feature_copies = {m: go(remote(features[m], f_peer.at[m], m, CORE_SUM, core_peer)) for m in (1, 0)}
 
     for m in (0, 1):
         ft[m] = features[m][...].T
+    for m in (1, 0):
+        feature_copies[m].wait_recv()
+        ft_peer[m] = f_peer[m].T
 
     down = lax.broadcasted_iota(jnp.int32, (rows, rows), 0)
     along = lax.broadcasted_iota(jnp.int32, (rows, rows), 1)
@@ -171,21 +175,20 @@
         copy.start()
         fg_copies.append(copy)
 
-    def share(m, xd, core):
-        left = ft[m, pl.ds(pl.multiple_of(xd * chunk, 16), chunk), :]
-        right = pgp[m, :, pl.ds(pl.multiple_of(core * CORE_STEP, 128), WINDOW)]
-        return jnp.dot(left, right, preferred_element_type=jnp.float32)
-
     core_copies, z_copies = {}, {}
 
-    def core_start(m, k):
-        core_out[m, k] = share(m, x_targets[k], 1 - c).astype(jnp.bfloat16)
-        core_copies[m, k] = go(remote(core_out.at[m, k], core_in.at[m, k], m, CORE_SUM + k, core_peer))
+    def window(core):
+        return pl.ds(pl.multiple_of(core * CORE_STEP, 128), WINDOW)
+
+    def core_start(m):
+        core_copies[m] = go(remote(pgp.at[m, :, window(1 - c)], pg_peer.at[m], m, CORE_SUM + 1, core_peer))
 
     def chip_share(m, k):
-        total = share(m, x_targets[k], c)
-        core_copies[m, k].wait_recv()
-        acc[m, k] = total + core_in[m, k].astype(jnp.float32)
+        block = pl.ds(pl.multiple_of(x_targets[k] * chunk, 16), chunk)
+        part = jnp.dot(ft[m, block, :], pgp[m, :, window(c)], preferred_element_type=jnp.float32)
+        if k == 0:
+            core_copies[m].wait_recv()
+        acc[m, k] = part + jnp.dot(ft_peer[m, block, :], pg_peer[m], preferred_element_type=jnp.float32)
 
     class Ring:
         def __init__(self, n, pair, value):
@@ -305,13 +308,10 @@
     arrived(1, 2)
     add(0, block_far, False)
     project_back(0)
-    core_start(0, 0)
-    core_start(0, 1)
-    core_start(0, 2)
+    core_start(0)
     chip_share(0, 0)
     ring_ix.relay(0)
     ring_ix.relay(1)
-    core_start(0, 3)
     chip_share(0, 1)
     ring_ix.direct(1)
     chip_share(0, 2)
@@ -326,14 +326,11 @@
     arrived(0, 2)
     add(1, block_far, False)
     project_back(1)
-    core_start(1, 0)
-    core_start(1, 1)
-    core_start(1, 2)
+    core_start(1)
     ring_ix.both()
     chip_share(1, 0)
     ring_tx.relay(0)
     ring_tx.relay(1)
-    core_start(1, 3)
     chip_share(1, 1)
     ring_ty.relay(0)
     ring_ty.direct(0)
@@ -425,8 +422,9 @@
             pltpu.VMEM((4, 1, rows), jnp.int32),
             pltpu.VMEM((2, rows, width), b16),
             pltpu.VMEM((2, rows, width), b16),
-            pltpu.VMEM((2, 4, chunk, WINDOW), b16),
-            pltpu.VMEM((2, 4, chunk, WINDOW), b16),
+            pltpu.VMEM((2, rows, depth), b16),
+            pltpu.VMEM((2, depth, rows), b16),
+            pltpu.VMEM((2, rows, WINDOW), b16),
             pltpu.VMEM((2, 4, chunk, WINDOW), f32),
             pltpu.VMEM((2, half, WINDOW), f32),
             pltpu.VMEM((2, rest, WINDOW), f32),

time: 63.9 us -> 63.6 us (level)
  no operation moved by 1% of the time
where the time goes in v5:
time: 63.6 us; the launch traced here: 63.5 us
  Pallas kernels  62.8 us (99%)
  between operations  0.64 us (1%)
    pallas_call x1, Pallas kernels, local(): pl.pallas_call(functools.partial(kernel, nz), out_shape=(jax.ShapeDtypeSt...  60.7 us
    pallas_call x1, Pallas kernels, local(): pl.pallas_call(hand_over, out_shape=[jax.ShapeDtypeStruct(out.shape, out....  2.11 us

profile of v5, /device:TPU:2, one launch (start us, length us, event | category | flops | bytes accessed | tf_op | source)
XLA Modules:
  0.0 63.5 jit_solution(14444206105817028243)
XLA Ops:
  0.6 60.7 %shard_map.84 = (bf16[192,1152]{1,0:T(8,128)(2,1)}, bf16[192,1152]{1,0:T(8,128)(2,1)}, f32[18,288]{1,0:T(8,128)}, f32[18,288]{1,0:T(8,128)}) custom-call(bf16[192,1152]{1,0:T(8,128)(2,1)} %f_i_hbm.1, bf16[192,1152]{1,0:T(8,128)(2,1)} %f_t_hbm.1, bf16[1152,1152]{1,0:T(8,128)(2,1)} %w_i_hbm.1, bf16[1152,1152]{1,0:T(8,128)(2,1)} %w_t_hbm.1, s32[1,192]{1,0:T(1,128)} %partner_hbm.1), custom_call_target="tpu_custom_call" | custom-call | flops 4499999744 | bytes 8000000 | tf_op jit(solution)/shard_map/pallas_call | solution.py:400
  61.3 2.1 %shard_map.85 = (bf16[192,1152]{1,0:T(8,128)(2,1)}, bf16[192,1152]{1,0:T(8,128)(2,1)}, f32[18,288]{1,0:T(8,128)}, f32[18,288]{1,0:T(8,128)}) custom-call(bf16[192,1152]{1,0:T(8,128)(2,1)} %get-tuple-element.8.a, bf16[192,1152]{1,0:T(8,128)(2,1)} %get-tuple-element.9.b, f32[18,288]{1,0:T(8,128)} %get-tuple-element.10.c, f32[18,288]{1,0:T(8,128)} %get-tuple-element.11.d), custom_call_target="tpu_custom_call" | custom-call | tf_op jit(solution)/shard_map/pallas_call | solution.py:449

commit v6 on v5

--- a/solution.py
+++ b/solution.py
@@ -18,18 +18,22 @@
 PART = 384
 PART_STEP = 256
 TILE = 16
+CUT = 80
 Y_FIRST = 64
 
 OWN_CORE, OWN_CHIP, FORWARD = 0, PIECES, 2 * PIECES
 CORE_SUM = 3 * PIECES
 Z_SUM = CORE_SUM + 2
-RINGS = 6
+RINGS = 4
+
+
+Z_ORDER = (4, 3, -3, 2, -2, 1, -1, 0)
 
 
 def kernel(nz, f_i_hbm, f_t_hbm, w_i_hbm, w_t_hbm, partner_hbm, fg_i_hbm, fg_t_hbm, wg_i, wg_t,
-           f_i, f_t, partner, fg, fg_sem, w, ft, proj, inv, grad, emb, pairs, pg, pgp,
-           f_peer, ft_peer, pg_peer, acc, sums_i, sums_t, sums_y, last, z_out, z_in, ring_bufs,
-           f_sem, w_sem, p_send, p_recv, send, recv, ring_send, ring_recv):
+           f_i, f_t, partner, fg, fg_sem, f_sem, w, ft, ft_z, proj, inv, grad, emb, pairs, pg, pgp,
+           f_peer, ft_peer, ft_z_peer, pg_peer, acc_i, acc, plane_out, plane_in, sums_t, sums_y, last, z_out, z_in,
+           long_bufs, ring_bufs, w_sem, p_send, p_recv, plane_send, plane_recv, send, recv, long_send, long_recv, ring_send, ring_recv):
     rows, depth = f_i.shape
     width = w.shape[2]
     chunk = depth // NX
@@ -58,7 +62,13 @@
     z_peers = [(lax.rem(z + d, nz), device(z=lax.rem(z + d, nz))) for d in range(1, nz)]
 
     barrier = pltpu.get_barrier_semaphore()
-    peers = [core_peer, chip_peer, far_peer, *x_pair, device(yh=1 - yh, yl=1 - yl)]
+    plane_peers = []
+    for dx in (2, 1, 3, 0):
+        for dy in (2, 1, 3, 0):
+            if dx or dy:
+                xd, yd = lax.rem(x + dx, NX), lax.rem(y + dy, 4)
+                plane_peers.append((xd * NYH + yd // 2, lax.rem(yd, 2), device(x=xd, yh=yd // 2, yl=lax.rem(yd, 2))))
+    peers = [core_peer, far_peer, *(peer for _, _, peer in plane_peers)]
     peers += [peer for _, peer in z_peers]
     for peer in peers:
         pl.semaphore_signal(barrier, inc=1, device_id=peer, device_id_type=pl.DeviceIdType.MESH)
@@ -102,11 +112,10 @@
             own[m, 0, k] = go(remote(ref, ref, m, OWN_CORE + k, core_peer))
             own[m, 1, k] = go(remote(ref, ref, m, OWN_CHIP + k, chip_peer))
 
-    def forward(m):
-        for k in range(PIECES):
-            own[m, 1, k].wait_recv()
-            ref = emb.at[m, block_chip, pl.ds(k * piece, piece)]
-            own[m, 2, k] = go(remote(ref, ref, m, FORWARD + k, core_peer))
+    def forward(m, k):
+        own[m, 1, k].wait_recv()
+        ref = emb.at[m, block_chip, pl.ds(k * piece, piece)]
+        own[m, 2, k] = go(remote(ref, ref, m, FORWARD + k, core_peer))
 
     def arrived(m, kind):
         for k in range(PIECES):
@@ -131,11 +140,19 @@
     send_own(0)
     feature_copies = {m: go(remote(features[m], f_peer.at[m], m, CORE_SUM, core_peer)) for m in (1, 0)}
 
-    for m in (0, 1):
-        ft[m] = features[m][...].T
-    for m in (1, 0):
-        feature_copies[m].wait_recv()
-        ft_peer[m] = f_peer[m].T
+    ft[...] = f_t[...].T
+    feature_copies[1].wait_recv()
+    ft_peer[...] = f_peer[1].T
+    feature_copies[0].wait_recv()
+    row = lax.broadcasted_iota(jnp.int32, (half, 1), 0)
+    source = (row // mine) * half + lax.rem(row, mine)
+    column = lax.broadcasted_iota(jnp.int32, (half, depth), 1)
+    for d in range(nz):
+        order = jnp.where(column == source + d * mine, 1.0, 0.0).astype(jnp.bfloat16)
+        for left, right in ((ft_z, f_i[...]), (ft_z_peer, f_peer[0])):
+            left[d] = lax.dot_general(
+                order, right, (((1,), (1,)), ((), ())), preferred_element_type=jnp.float32
+            ).astype(jnp.bfloat16)
 
     down = lax.broadcasted_iota(jnp.int32, (rows, rows), 0)
     along = lax.broadcasted_iota(jnp.int32, (rows, rows), 1)
@@ -184,11 +201,47 @@
         core_copies[m] = go(remote(pgp.at[m, :, window(1 - c)], pg_peer.at[m], m, CORE_SUM + 1, core_peer))
 
     def chip_share(m, k):
-        block = pl.ds(pl.multiple_of(x_targets[k] * chunk, 16), chunk)
-        part = jnp.dot(ft[m, block, :], pgp[m, :, window(c)], preferred_element_type=jnp.float32)
+        if m == 0:
+            place = lax.rem(z + Z_ORDER[k] + nz, nz)
+            own_left, peer_left, total = ft_z[place], ft_z_peer[place], acc_i
+        else:
+            block = pl.ds(pl.multiple_of(x_targets[k] * chunk, 16), chunk)
+            own_left, peer_left, total = ft[block, :], ft_peer[block, :], acc
+        part = jnp.dot(own_left, pgp[m, :, window(c)], preferred_element_type=jnp.float32)
         if k == 0:
             core_copies[m].wait_recv()
-        acc[m, k] = part + jnp.dot(ft_peer[m, block, :], pg_peer[m], preferred_element_type=jnp.float32)
+        total[k] = part + jnp.dot(peer_left, pg_peer[m], preferred_element_type=jnp.float32)
+
+    z_pair = (device(z=lax.rem(z + 1, nz)), device(z=lax.rem(z + nz - 1, nz)))
+    spans = (pl.ds(0, CUT), pl.ds(CUT, half - CUT))
+    long_copies = {}
+
+    def own_part(d, h):
+        return acc_i[Z_ORDER.index(d), spans[h], :]
+
+    def long_push(way, hops, far):
+        h = way if far else 1 - way
+        out, into = long_bufs[way][h]
+        value = own_part(hops if way == 0 or hops == nz // 2 else -hops, h)
+        first = nz // 2 if far else nz // 2 - 1
+        if hops < first:
+            value = value + long_pull(way, hops + 1, far)
+        slot = first - hops
+        out[slot] = value.astype(jnp.bfloat16)
+        s = 2 * slot + (0 if far else 1)
+        long_copies[way, hops, far] = go(pltpu.make_async_remote_copy(
+            src_ref=out.at[slot], dst_ref=into.at[slot], send_sem=long_send.at[way, s], recv_sem=long_recv.at[way, s],
+            device_id=z_pair[way], device_id_type=pl.DeviceIdType.MESH))
+
+    def long_pull(way, hops, far):
+        long_copies[way, hops, far].wait_recv()
+        h = way if far else 1 - way
+        first = nz // 2 if far else nz // 2 - 1
+        return long_bufs[way][h][1][first - hops].astype(jnp.float32)
+
+    def long_step(hops, far):
+        for way in range(2):
+            long_push(way, hops, far)
 
     class Ring:
         def __init__(self, n, pair, value):
@@ -220,8 +273,8 @@
         def total(self, h):
             return self.value(3, h) + self.pull(h, 1) + self.pull(h, 2)
 
-    def x_first(m, low):
-        return lambda k, h: acc[m, k, h * half + low:(h + 1) * half, :]
+    def x_first(k, h):
+        return acc[k, h * half + Y_FIRST:(h + 1) * half, :]
 
     def column_part(l):
         return pl.ds(pl.multiple_of(l * PART_STEP, 128), PART)
@@ -235,19 +288,17 @@
     def y_first(k, h):
         t = y_targets[k]
         block = pl.ds(pl.multiple_of((t // 2) * half, 8), Y_FIRST)
-        return acc[1, 2 * h:2 * h + 2, block, column_part(lax.rem(t, 2))]
+        return acc[2 * h:2 * h + 2, block, column_part(lax.rem(t, 2))]
 
     def x_second(k, h):
         n = Y_FIRST // 2
         return sums_y[k, h * n:(h + 1) * n, :]
 
-    cuts_i, cuts_t = (0, 80, half), (0, 48, half - Y_FIRST)
-    ring_ix = Ring(0, x_pair, x_first(0, 0))
-    ring_iy = Ring(1, y_pair, y_second(sums_i, cuts_i))
-    ring_tx = Ring(2, x_pair, x_first(1, Y_FIRST))
-    ring_txy = Ring(3, y_pair, y_second(sums_t, cuts_t))
-    ring_ty = Ring(4, y_pair, y_first)
-    ring_tyx = Ring(5, x_pair, x_second)
+    cuts_t = (0, 48, half - Y_FIRST)
+    ring_tx = Ring(0, x_pair, x_first)
+    ring_txy = Ring(1, y_pair, y_second(sums_t, cuts_t))
+    ring_ty = Ring(2, y_pair, y_first)
+    ring_tyx = Ring(3, x_pair, x_second)
 
     def begin(ring):
         ring.relay(0)
@@ -259,40 +310,75 @@
     segments = quarter // spare
     rest = mine - TILE
 
-    def z_start(m):
-        total = last[m]
-        offset = (quarter - PART_STEP) * (yl + 2 * c)
-        total = pltpu.roll(total, lax.rem(PART - offset, PART), 1)
-        row = lax.broadcasted_iota(jnp.int32, (nz * TILE, half), 0)
-        column = lax.broadcasted_iota(jnp.int32, (nz * TILE, half), 1)
+    def offset_of(l):
+        return (quarter - PART_STEP) * (l + 2 * c)
+
+    def pack(total, l):
+        total = total.astype(jnp.bfloat16)
+        row = lax.broadcasted_iota(jnp.int32, (8 * TILE, half), 0)
+        column = lax.broadcasted_iota(jnp.int32, (8 * TILE, half), 1)
         which, within = row // TILE, lax.rem(row, TILE)
 
-        def pick(chosen, source, value):
+        def pick(chosen, source):
             spread = jnp.where(chosen & (column == which * mine + source), 1.0, 0.0).astype(jnp.bfloat16)
-            return jnp.dot(spread, value.astype(jnp.bfloat16), preferred_element_type=jnp.float32)
-
-        body = pick(within < TILE, within, total)
-        tail = jnp.zeros_like(body)
-        for s in range(segments):
-            moved = pltpu.roll(total, quarter - s * spare, 1)
-            chosen = (within < rest * segments) & (lax.rem(within, segments) == s)
-            tail = tail + pick(chosen, TILE + within // segments, moved)
-        lane = lax.broadcasted_iota(jnp.int32, body.shape, 1)
-        packed = jnp.where(lane < quarter, body, tail).astype(jnp.bfloat16)
-        for d in range(nz):
-            z_out[m, d] = packed[d * TILE:(d + 1) * TILE]
-        for s, (zd, peer) in enumerate(z_peers):
-            z_copies[m, s] = go(remote(z_out.at[m, zd], z_in.at[m, s], m, Z_SUM + s, peer))
-
-    def z_finish(m, out):
-        total = z_out[m, z].astype(jnp.float32)
-        for s in range(nz - 1):
-            z_copies[m, s].wait_recv()
-            total = total + z_in[m, s].astype(jnp.float32)
+            return jnp.dot(spread, total, preferred_element_type=jnp.float32)
+
+        body = pick(within < TILE, within)
+        tail = pick(within < rest * segments, TILE + within // segments)
+        row = lax.broadcasted_iota(jnp.int32, (8 * TILE, 1), 0)
+        segment = lax.rem(lax.rem(row, TILE), segments)
+        moved = [pltpu.roll(tail, quarter - s * spare, 1) for s in range(segments)]
+        chosen = moved[0]
+        for s in range(1, segments):
+            chosen = jnp.where(segment == s, moved[s], chosen)
+        lane = lax.rem(lax.broadcasted_iota(jnp.int32, body.shape, 1) + PART - offset_of(l), PART)
+        return jnp.where(lane < quarter, body, chosen).astype(jnp.bfloat16)
+
+    def unpack(total, out):
+        total = pltpu.roll(total, lax.rem(PART - offset_of(yl), PART), 1)
         out[:TILE, :] = total[:, :quarter]
         for r in range(rest):
-            rows_of = [total[r * segments + s:r * segments + s + 1, quarter:] for s in range(segments)]
-            out[TILE + r:TILE + r + 1, :] = jnp.concatenate(rows_of, axis=1)
+            pieces = [total[r * segments + s:r * segments + s + 1, quarter:] for s in range(segments)]
+            out[TILE + r:TILE + r + 1, :] = jnp.concatenate(pieces, axis=1)
+
+    plane_copies = []
+
+    def plane_pack():
+        low = own_part(0, 0) + long_pull(0, 1, True) + long_pull(1, 1, False)
+        high = own_part(0, 1) + long_pull(0, 1, False) + long_pull(1, 1, True)
+        total = jnp.concatenate([low, high], axis=0)
+        for l in range(2):
+            packed = pack(total[:, l * PART_STEP:l * PART_STEP + PART], l)
+            for d in range(8):
+                plane_out[l, d] = packed[d * TILE:(d + 1) * TILE]
+
+    def plane_start():
+        for s, (place, l, peer) in enumerate(plane_peers):
+            plane_copies.append(go(pltpu.make_async_remote_copy(
+                src_ref=plane_out.at[l, place], dst_ref=plane_in.at[s],
+                send_sem=plane_send.at[s], recv_sem=plane_recv.at[s],
+                device_id=peer, device_id_type=pl.DeviceIdType.MESH)))
+
+    def plane_finish(out):
+        total = plane_out[yl, x * NYH + yh].astype(jnp.float32)
+        for s, copy in enumerate(plane_copies):
+            copy.wait_recv()
+            total = total + plane_in[s].astype(jnp.float32)
+        unpack(total, out)
+
+    def z_start():
+        packed = pack(last[...], yl)
+        for d in range(nz):
+            z_out[d] = packed[d * TILE:(d + 1) * TILE]
+        for s, (zd, peer) in enumerate(z_peers):
+            z_copies[s] = go(remote(z_out.at[zd], z_in.at[s], 1, Z_SUM + s, peer))
+
+    def z_finish(out):
+        total = z_out[z].astype(jnp.float32)
+        for s in range(nz - 1):
+            z_copies[s].wait_recv()
+            total = total + z_in[s].astype(jnp.float32)
+        unpack(total, out)
 
     add = add_block
     add(0, narrow, True)
@@ -303,31 +389,34 @@
     arrived(0, 0)
     add(1, block_core, False)
 
-    forward(1)
+    forward(1, 0)
+    forward(1, 1)
     add(0, block_chip, False)
     arrived(1, 2)
     add(0, block_far, False)
     project_back(0)
+    half_z = nz // 2
     core_start(0)
     chip_share(0, 0)
-    ring_ix.relay(0)
-    ring_ix.relay(1)
-    chip_share(0, 1)
-    ring_ix.direct(1)
-    chip_share(0, 2)
-    ring_ix.direct(0)
-    chip_share(0, 3)
+    long_step(half_z, True)
+    for way in range(2):
+        chip_share(0, 1 + way)
+        long_push(way, half_z - 1, False)
+    for k in range(3, nz):
+        chip_share(0, k)
+    forward(0, 0)
     feature_grad(0, fg_i_hbm)
-
-    forward(0)
+    long_step(3, True)
+
+    forward(0, 1)
     pair_copies[1].wait_recv()
     pair_copies[2].wait_recv()
+    long_step(2, False)
     add(1, block_chip, False)
     arrived(0, 2)
     add(1, block_far, False)
     project_back(1)
     core_start(1)
-    ring_ix.both()
     chip_share(1, 0)
     ring_tx.relay(0)
     ring_tx.relay(1)
@@ -337,16 +426,15 @@
     ring_tx.direct(1)
     chip_share(1, 2)
     ring_tx.direct(0)
+    long_step(2, True)
     chip_share(1, 3)
     ring_ty.relay(1)
     ring_ty.direct(1)
-
-    for h in range(2):
-        sums_i[h] = ring_ix.total(h)
-    begin(ring_iy)
+    long_step(1, False)
+    long_step(1, True)
+
     ring_tx.both()
     ring_ty.both()
-    ring_iy.both()
     feature_grad(1, fg_t_hbm)
     for h in range(2):
         sums_t[h] = ring_tx.total(h)
@@ -354,19 +442,18 @@
     for h in range(2):
         sums_y[2 * h:2 * h + 2] = ring_ty.total(h)
     begin(ring_tyx)
-    for h in range(2):
-        last[0, cuts_i[h]:cuts_i[h + 1]] = ring_iy.total(h)
-    z_start(0)
+    plane_pack()
     ring_txy.both()
     ring_tyx.both()
+    plane_start()
     for h in range(2):
         n = Y_FIRST // 2
-        last[1, h * n:(h + 1) * n] = ring_tyx.total(h)
+        last[h * n:(h + 1) * n] = ring_tyx.total(h)
     for h in range(2):
-        last[1, Y_FIRST + cuts_t[h]:Y_FIRST + cuts_t[h + 1]] = ring_txy.total(h)
-    z_start(1)
-    z_finish(0, wg_i)
-    z_finish(1, wg_t)
+        last[Y_FIRST + cuts_t[h]:Y_FIRST + cuts_t[h + 1]] = ring_txy.total(h)
+    z_start()
+    plane_finish(wg_i)
+    z_finish(wg_t)
     for copy in fg_copies:
         copy.wait()
     for copy in started:
@@ -389,14 +476,17 @@
     copies = Z_SUM + nz - 1
     rest = half - Y_FIRST
     ring_shapes = [
-        ((half, WINDOW), (half, WINDOW)),
-        ((80, PART), (half - 80, PART)),
         ((rest, WINDOW), (rest, WINDOW)),
         ((48, PART), (rest - 48, PART)),
         ((2, Y_FIRST, PART), (2, Y_FIRST, PART)),
         ((Y_FIRST // 2, PART), (Y_FIRST // 2, PART)),
     ]
     rings = [[[pltpu.VMEM((3, *shape), b16) for _ in range(2)] for shape in pair] for pair in ring_shapes]
+    long_rows, hops = (CUT, half - CUT), nz // 2
+    longs = [
+        [[pltpu.VMEM((hops if h == way else hops - 1, long_rows[h], WINDOW), b16) for _ in range(2)] for h in range(2)]
+        for way in range(2)
+    ]
     outs = pl.pallas_call(
         functools.partial(kernel, nz),
         out_shape=(
@@ -413,8 +503,10 @@
             pltpu.VMEM((1, rows), jnp.int32),
             pltpu.VMEM((2, rows, depth), b16),
             pltpu.SemaphoreType.DMA((2,)),
+            pltpu.SemaphoreType.DMA((3,)),
             pltpu.VMEM((2, depth, width), b16),
-            pltpu.VMEM((2, depth, rows), b16),
+            pltpu.VMEM((depth, rows), b16),
+            pltpu.VMEM((nz, half, rows), b16),
             pltpu.VMEM((2, rows, width), f32),
             pltpu.VMEM((2, rows, 1), f32),
             pltpu.VMEM((2, rows, width), f32),
@@ -423,22 +515,29 @@
             pltpu.VMEM((2, rows, width), b16),
             pltpu.VMEM((2, rows, width), b16),
             pltpu.VMEM((2, rows, depth), b16),
-            pltpu.VMEM((2, depth, rows), b16),
+            pltpu.VMEM((depth, rows), b16),
+            pltpu.VMEM((nz, half, rows), b16),
             pltpu.VMEM((2, rows, WINDOW), b16),
-            pltpu.VMEM((2, 4, chunk, WINDOW), f32),
-            pltpu.VMEM((2, half, WINDOW), f32),
+            pltpu.VMEM((nz, half, WINDOW), f32),
+            pltpu.VMEM((4, chunk, WINDOW), f32),
+            pltpu.VMEM((2, 8, TILE, PART), b16),
+            pltpu.VMEM((15, TILE, PART), b16),
             pltpu.VMEM((2, rest, WINDOW), f32),
             pltpu.VMEM((4, Y_FIRST, PART), f32),
-            pltpu.VMEM((2, half, PART), f32),
-            pltpu.VMEM((2, nz, TILE, PART), b16),
-            pltpu.VMEM((2, nz - 1, TILE, PART), b16),
+            pltpu.VMEM((half, PART), f32),
+            pltpu.VMEM((nz, TILE, PART), b16),
+            pltpu.VMEM((nz - 1, TILE, PART), b16),
+            longs,
             rings,
-            pltpu.SemaphoreType.DMA((3,)),
             pltpu.SemaphoreType.DMA((2,)),
             pltpu.SemaphoreType.DMA((3,)),
             pltpu.SemaphoreType.DMA((3,)),
+            pltpu.SemaphoreType.DMA((15,)),
+            pltpu.SemaphoreType.DMA((15,)),
             pltpu.SemaphoreType.DMA((2, copies)),
             pltpu.SemaphoreType.DMA((2, copies)),
+            pltpu.SemaphoreType.DMA((2, 7)),
+            pltpu.SemaphoreType.DMA((2, 7)),
             pltpu.SemaphoreType.DMA((RINGS, 6)),
             pltpu.SemaphoreType.DMA((RINGS, 6)),
         ],

time: 63.6 us -> 63.9 us (level)
  no operation moved by 1% of the time
where the time goes in v6:
time: 63.9 us; the launch traced here: 63.4 us
  Pallas kernels  62.7 us (98%)
  between operations  0.64 us (1%)
    pallas_call x1, Pallas kernels, local(): pl.pallas_call(functools.partial(kernel, nz), out_shape=(jax.ShapeDtypeSt...  60.6 us
    pallas_call x1, Pallas kernels, local(): pl.pallas_call(hand_over, out_shape=[jax.ShapeDtypeStruct(out.shape, out....  2.11 us

profile of v6, /device:TPU:2, one launch (start us, length us, event | category | flops | bytes accessed | tf_op | source)
XLA Modules:
  0.0 63.4 jit_solution(9005409959551051714)
XLA Ops:
  0.6 60.6 %shard_map.84 = (bf16[192,1152]{1,0:T(8,128)(2,1)}, bf16[192,1152]{1,0:T(8,128)(2,1)}, f32[18,288]{1,0:T(8,128)}, f32[18,288]{1,0:T(8,128)}) custom-call(bf16[192,1152]{1,0:T(8,128)(2,1)} %f_i_hbm.1, bf16[192,1152]{1,0:T(8,128)(2,1)} %f_t_hbm.1, bf16[1152,1152]{1,0:T(8,128)(2,1)} %w_i_hbm.1, bf16[1152,1152]{1,0:T(8,128)(2,1)} %w_t_hbm.1, s32[1,192]{1,0:T(1,128)} %partner_hbm.1), custom_call_target="tpu_custom_call" | custom-call | flops 4499999744 | bytes 8000000 | tf_op jit(solution)/shard_map/pallas_call | solution.py:490
  61.3 2.1 %shard_map.85 = (bf16[192,1152]{1,0:T(8,128)(2,1)}, bf16[192,1152]{1,0:T(8,128)(2,1)}, f32[18,288]{1,0:T(8,128)}, f32[18,288]{1,0:T(8,128)}) custom-call(bf16[192,1152]{1,0:T(8,128)(2,1)} %get-tuple-element.8.a, bf16[192,1152]{1,0:T(8,128)(2,1)} %get-tuple-element.9.b, f32[18,288]{1,0:T(8,128)} %get-tuple-element.10.c, f32[18,288]{1,0:T(8,128)} %get-tuple-element.11.d), custom_call_target="tpu_custom_call" | custom-call | tf_op jit(solution)/shard_map/pallas_call | solution.py:548
